TPU v7x, 32 devices: a whole 2x2x4 slice. The times are simulated.
32 devices in a mesh: role: 4 (over y, x), atoms: 8 (over z, core).
Axes of the slice: x: 2, y: 2, z: 4, core: 2. Of those that a mesh axis runs over, the one named last changes fastest.
Arguments:
- features: bfloat16 [4, 8, 256, 256], P('role', 'atoms'), may hold values from -6 to 6
- positions: float32 [4, 8, 3, 256], P('role', 'atoms'), may hold values from 0 to 1, as said below
- neighbours: int32 [4, 8, 32, 256], P('role', 'atoms'), may hold values from 0 to 2304, as said below
- images: int32 [4, 8, 32, 256], P('role', 'atoms'), may hold values from 0 to 26
- wave: int32 [3, 2048], replicated, may hold values from -8 to 8, as said below
- kgain: float32 [256], replicated, may hold values from 0.5 to 4
- w_in: bfloat16 [256, 256], replicated, may hold values from -0.375 to 0.375
- w_query: bfloat16 [256, 256], replicated, may hold values from -0.375 to 0.375
- w_rbf: bfloat16 [64, 256], replicated, may hold values from -1.5 to 1.5
- b_rbf: float32 [256], replicated, may hold values from -4 to 4
- w_filter: bfloat16 [256, 256], replicated, may hold values from -0.375 to 0.375
- w_out: bfloat16 [256, 256], replicated, may hold values from -0.375 to 0.375
Outputs:
- updated: bfloat16 [4, 8, 256, 256], P('role', 'atoms')
Inputs may be any that keep to these rules, and one draw needn't show every extreme that they name: `neighbours`: an entry (p * 3 + q) * 256 + t names atom t of the brick offset by p - 1 along the first and q - 1 along the second brick dimension, periodically; 2304 marks an empty slot. Empty slots come last; every list has 16 or more entries, and every brick has a full list. `positions`: atom coordinates of brick (a, b) lie in [a / 4, (a + 1) / 4) x [b / 8, (b + 1) / 8) x [0, 1). No wave vector has all three indices zero.
All inputs are finite; a program needn't handle non-finite values.
Results may differ from a plain program's by a relative error of at most 0.0085.
Values may be sent and summed in bfloat16 or wider, within the bound.
A program may use at most 128 MiB of HBM per device.

v0:
```python
import math

import jax
import jax.numpy as jnp
from jax import lax
from jax.sharding import PartitionSpec as P

box_side = 1.0
soft_sq = 0.01
damping = 64.0
ewald_scale = 0.25


def padded(block, sides, width):
    for axis, dim in sides:
        count = lax.axis_size(axis)
        forward = [(i, i + 1) for i in range(count - 1)]
        forward.append((count - 1, 0))
        backward = [(target, source) for source, target in forward]
        low = lax.ppermute(
            lax.slice_in_dim(block, block.shape[dim] - width, None, axis=dim), axis, forward
        )
        high = lax.ppermute(lax.slice_in_dim(block, 0, width, axis=dim), axis, backward)
        block = jnp.concatenate([low, block, high], axis=dim)
    return block


def shifted_softplus(values):
    return jax.nn.softplus(values) - math.log(2.0)


def block_messages(
    near_table, near_coords, own_pos, near_slots, near_images, w_rbf, b_rbf, w_filter
):
    slot_count, atom_count = near_slots.shape
    flat_slots = near_slots.reshape(-1)
    near_pos = jnp.take(near_coords, flat_slots, axis=1).reshape(3, slot_count, atom_count)
    delta_first = (
        near_pos[0] + (near_images // 9 - 1).astype(jnp.float32) * box_side - own_pos[0][None, :]
    )
    delta_second = (
        near_pos[1]
        + (near_images // 3 % 3 - 1).astype(jnp.float32) * box_side
        - own_pos[1][None, :]
    )
    delta_third = (
        near_pos[2] + (near_images % 3 - 1).astype(jnp.float32) * box_side - own_pos[2][None, :]
    )
    distance = jnp.sqrt(
        delta_first * delta_first
        + delta_second * delta_second
        + delta_third * delta_third
        + soft_sq
    )
    basis_count = w_rbf.shape[0]
    centers = jnp.arange(basis_count, dtype=jnp.float32) * (4.0 / (basis_count - 1))
    sharpness = (basis_count / 4.0) ** 2
    basis = jnp.exp(-sharpness * (distance.reshape(-1, 1) - centers[None, :]) ** 2).astype(
        jnp.bfloat16
    )
    inner = shifted_softplus(
        jnp.dot(basis, w_rbf, preferred_element_type=jnp.float32) + b_rbf
    ).astype(jnp.bfloat16)
    filters = jnp.dot(inner, w_filter, preferred_element_type=jnp.float32)
    gathered = jnp.take(near_table, flat_slots, axis=0)
    return (filters * gathered).reshape(slot_count, atom_count, -1).sum(axis=0)


def phase_tables(own_pos, wave):
    vectors = wave.astype(jnp.float32) * (2.0 * math.pi / box_side)
    angle = lax.dot_general(
        own_pos, vectors, (((0,), (0,)), ((), ())), precision=lax.Precision.HIGHEST
    )
    return (jnp.cos(angle).astype(jnp.bfloat16), jnp.sin(angle).astype(jnp.bfloat16))


def wave_filter(wave, kgain):
    squares = jnp.sum(wave.astype(jnp.float32) ** 2, axis=0)
    return ewald_scale * kgain[None, :] * (jnp.exp(-squares / damping) / squares)[:, None]


def contract_rows(left_side, right_side):
    return lax.dot_general(
        left_side, right_side, (((0,), (0,)), ((), ())), preferred_element_type=jnp.float32
    )


def local(
    features,
    positions,
    neighbours,
    images,
    wave,
    kgain,
    w_in,
    w_query,
    w_rbf,
    b_rbf,
    w_filter,
    w_out,
):
    own_rows = features[0, 0]
    atom_count = own_rows.shape[0]
    feat_width = own_rows.shape[1]
    devices = lax.axis_size(("role", "atoms"))
    atom_total = atom_count * devices
    hidden_x = jnp.dot(own_rows, w_in, preferred_element_type=jnp.float32).astype(jnp.bfloat16)
    window, places = (
        padded(hidden_x[None, None], (("role", 0), ("atoms", 1)), 1),
        padded(positions.astype(jnp.bfloat16), (("role", 0), ("atoms", 1)), 1).astype(
            positions.dtype
        ),
    )
    near_table = jnp.concatenate(
        [window.reshape(9 * atom_count, feat_width), jnp.zeros((1, feat_width), jnp.bfloat16)],
        axis=0,
    )
    coord_rows = jnp.transpose(places, (2, 0, 1, 3)).reshape(3, 9 * atom_count)
    near_coords = jnp.concatenate([coord_rows, jnp.zeros((3, 1), jnp.float32)], axis=1)
    own_pos = positions[0, 0]
    own_slots = neighbours[0, 0]
    own_images = images[0, 0]
    block_size = min(atom_count, 512)
    groups = atom_count // block_size

    def one_block(block):
        return block_messages(
            near_table, near_coords, own_pos, own_slots, own_images, w_rbf, b_rbf, w_filter
        )

    short_msg = lax.map(one_block, jnp.arange(groups, dtype=jnp.int32)).reshape(
        atom_count, feat_width
    )
    queries = jnp.dot(own_rows, w_query, preferred_element_type=jnp.float32).astype(jnp.bfloat16)
    cosine, sine = phase_tables(own_pos, wave)
    partials = jnp.stack(
        [contract_rows(cosine, queries), contract_rows(sine, queries)]
    ) * atom_total ** (-0.5)
    k_filter = wave_filter(wave, kgain)
    totals = lax.psum(partials, ("role", "atoms"))
    filtered = (totals * k_filter[None]).astype(jnp.bfloat16)
    ewald = jnp.dot(cosine, filtered[0], preferred_element_type=jnp.float32) + jnp.dot(
        sine, filtered[1], preferred_element_type=jnp.float32
    )
    combined = (short_msg * own_slots.shape[0] ** (-0.5) + ewald).astype(jnp.bfloat16)
    result = (
        own_rows.astype(jnp.float32) + jnp.dot(combined, w_out, preferred_element_type=jnp.float32)
    ).astype(jnp.bfloat16)
    return result[None, None]


def solution(mesh):
    in_specs = (
        P("role", "atoms", None, None),
        P("role", "atoms", None, None),
        P("role", "atoms", None, None),
        P("role", "atoms", None, None),
        P(),
        P(),
        P(),
        P(),
        P(),
        P(),
        P(),
        P(),
    )
    out_specs = P("role", "atoms", None, None)
    return jax.shard_map(local, mesh=mesh, in_specs=in_specs, out_specs=out_specs, check_vma=False)
```

profile of v0, /device:TPU:0, one launch (start us, length us, event | category | flops | bytes accessed | tf_op | source)
XLA Modules:
  0.0 210.5 jit_solution(1667292143750977789)
XLA Ops:
  6.5 0.7 convert_element_type.71
  7.3 2.9 %collective-permute-start = (bf16[1,1,3,256]{3,1,2,0:T(2,128)(2,1)S(1)}, bf16[1,1,3,256]{3,1,2,0:T(2,128)(2,1)S(1)}, u32[]{:S(2)}, u32[]{:S(2)}) collective-permute-start(bf16[1,1,3,256]{3,1,2,0:T(2,128)(2,1)S(1)} %convert_element_type.71), channel_id=1, source_target_pairs={{0,8},{8,16},{16,24},{24,0},{1,9},{9,17},{17,25},{25,1},{2,10},{10... | collective-permute-start | bytes 4616 | tf_op jit(solution)/shard_map/ppermute | solution.py:20
  10.2 1.0 collective-permute-start.1
  11.2 1.8 fusion.6
  13.0 1.1 collective-permute-start.4
  14.1 1.9 collective-permute-start.5
  15.9 2.6 %fusion.38 = f32[2048,256]{1,0:T(8,128)S(1)} fusion(s32[3,2048]{1,0:T(4,128)} %param.16, f32[1,1,3,256]{3,1,2,0:T(1,128)} %param.13), kind=kOutput, calls=%fused_computation.68 | convolution fusion | flops 18886656 | bytes 2124800 | tf_op jit(solution)/shard_map/dot_general | solution.py:71
  18.8 9.1 %convolution_bitcast_fusion = f32[1,2048,256]{2,1,0:T(8,128)S(1)} fusion(bf16[256,256]{1,0:T(8,128)(2,1)S(1)} %convolution_convert_fusion, f32[2048,256]{1,0:T(8,128)S(1)} %fusion.38), kind=kOutput, calls=%fused_computation.13 | convolution fusion | flops 268959744 | bytes 4325376 | tf_op jit(solution)/shard_map/dot_general | solution.py:83
  27.9 9.0 %convolution_bitcast_fusion.1 = f32[1,2048,256]{2,1,0:T(8,128)S(1)} fusion(bf16[256,256]{1,0:T(8,128)(2,1)S(1)} %convolution_convert_fusion, f32[2048,256]{1,0:T(8,128)S(1)} %fusion.38), kind=kOutput, calls=%fused_computation.14 | convolution fusion | flops 268959744 | bytes 4325376 | tf_op jit(solution)/shard_map/dot_general | solution.py:83
  36.9 2.3 %maximum_multiply_fusion = f32[2,2048,256]{2,1,0:T(8,128)} fusion(f32[1,2048,256]{2,1,0:T(8,128)S(1)} %convolution_bitcast_fusion, f32[1,2048,256]{2,1,0:T(8,128)S(1)} %convolution_bitcast_fusion.1), kind=kLoop, calls=%fused_computation.10 | loop fusion | flops 2097152 | bytes 8388608 | tf_op jit(solution)/shard_map/mul | solution.py:136
  39.2 0.6 copy-done.14
  40.9 1.7 broadcast_multiply_fusion
  42.7 3.5 %collective-permute-start.3 = (bf16[3,1,3,256]{3,1,2,0:T(2,128)(2,1)S(1)}, bf16[3,1,3,256]{3,1,2,0:T(2,128)(2,1)S(1)}, u32[]{:S(2)}, u32[]{:S(2)}) collective-permute-start(bf16[3,1,3,256]{3,1,2,0:T(2,128)(2,1)S(1)} %pad_maximum_fusion.2), channel_id=1, source_target_pairs={{1,0},{2,1},{3,2},{4,3},{5,4},{6,5},{7,6},{0,7},{9,8},{10,9},{11,1... | collective-permute-start | bytes 13832 | tf_op jit(solution)/shard_map/ppermute | solution.py:23
  49.8 0.6 copy.24
  51.7 1.1 copy.15
  52.8 1.1 pad_convert_fusion
  54.0 30.5 %gather_fusion = f32[8192,3]{1,0:T(8,128)} fusion(f32[3,2305]{0,1:T(8,128)S(1)} %pad_convert_fusion, s32[8192]{0:T(1024)} %broadcast_clamp_fusion), kind=kCustom, calls=%fused_computation | custom fusion | bytes 229376 | tf_op jit(solution)/shard_map/while/body/eval_jaxpr/jit(_take)/gather | solution.py:37
  84.5 6.2 %select_bitcast_fusion = f32[3,8192]{0,1:T(8,128)S(1)} fusion(f32[8192,3]{1,0:T(8,128)} %gather_fusion, pred[8192]{0:T(1024)(128)(4,1)S(1)} %compare_and_fusion), kind=kLoop, calls=%fused_computation.11 | loop fusion | flops 24576 | bytes 204800 | tf_op jit(solution)/shard_map/while/body/eval_jaxpr/jit(_take)/select_n | solution.py:37
  90.8 1.1 pad_maximum_fusion.1
  92.0 3.5 %collective-permute-start.7 = (bf16[3,1,256,256]{3,2,1,0:T(8,128)(2,1)S(1)}, bf16[3,1,256,256]{3,2,1,0:T(8,128)(2,1)S(1)}, u32[]{:S(2)}, u32[]{:S(2)}) collective-permute-start(bf16[3,1,256,256]{3,2,1,0:T(8,128)(2,1)S(1)} %pad_maximum_fusion.1), channel_id=1, source_target_pairs={{1,0},{2,1},{3,2},{4,3},{5,4},{6,5},{7,6},{0,7},{9,8},{10,9},{11,1... | collective-permute-start | bytes 1179656 | tf_op jit(solution)/shard_map/ppermute | solution.py:23
  95.6 5.5 %slice_reduce_fusion = (f32[8192]{0:T(1024)S(1)}, f32[8192]{0:T(1024)S(1)}, f32[8192]{0:T(1024)S(1)}) fusion(f32[3,8192]{0,1:T(8,128)S(1)} %select_bitcast_fusion), kind=kLoop, calls=%fused_computation.7 | loop fusion | bytes 196608 | tf_op jit(solution)/shard_map/while/body/eval_jaxpr/slice | solution.py:47
  101.1 0.7 fusion.26
  101.8 3.6 %collective-permute-done.6 = bf16[3,1,256,256]{3,2,1,0:T(8,128)(2,1)S(1)} collective-permute-done((bf16[3,1,256,256]{3,2,1,0:T(8,128)(2,1)S(1)}, bf16[3,1,256,256]{3,2,1,0:T(8,128)(2,1)S(1)}, u32[]{:S(2)}, u32[]{:S(2)}) %collective-permute-start.6) | collective-permute-done | bytes 393248 | tf_op jit(solution)/shard_map/ppermute | solution.py:20
  105.5 1.2 pad_maximum_fusion
  106.7 35.7 %gather_fusion.1 = bf16[8192,256]{1,0:T(8,128)(2,1)} fusion(bf16[2305,256]{1,0:T(8,128)(2,1)S(1)} %concatenate.26, s32[8192]{0:T(1024)} %broadcast_clamp_fusion), kind=kCustom, calls=%fused_computation.1 | custom fusion | bytes 8421376 | tf_op jit(solution)/shard_map/while/body/eval_jaxpr/jit(_take)/gather | solution.py:65
  142.5 10.3 %convolution_multiply_fusion = f32[8192,256]{1,0:T(8,128)} fusion(bf16[256,256]{1,0:T(8,128)(2,1)S(1)} %copy-done, bf16[8192,256]{1,0:T(8,128)(2,1)} %gather_fusion.1, pred[8192]{0:T(1024)(128)(4,1)S(1)} %compare_and_fusion, bf16[64,256]{1,0:T(8,128)(2,1)} %param.20, f32[256]{0:T(256)S(1)} %copy-done.18, f32[64]{0:T(128)} %iota_multiply_fusion, f32[8192]{0:T(1024)} %fusion.26), kind=kOutput, calls=%fused_computation.3 | convolution fusion | flops 1369440256 | bytes 12788992 | tf_op jit(solution)/shard_map/while/body/eval_jaxpr/dot_general | solution.py:64
  152.8 4.5 %reduce_sum.19 = f32[256,256]{1,0:T(8,128)S(1)} reduce(f32[32,256,256]{2,1,0:T(8,128)} %bitcast.71, f32[]{:T(128)} %constant.102.clone.1), dimensions={0}, to_apply=%region_0.1 | reduce | flops 2031616 | bytes 8650756 | tf_op jit(solution)/shard_map/while/body/eval_jaxpr/reduce_sum | solution.py:66
  157.3 25.7 %all-reduce.4.cloned.1.call-done = f32[2,2048,256]{2,1,0:T(8,128)} async-done(((f32[2,2048,256]{2,1,0:T(8,128)}), f32[2,2048,256]{2,1,0:T(8,128)}) %all-reduce.4.cloned.1.call-update) | async-done | bytes 4194320 | tf_op jit(solution)/shard_map/psum | solution.py:140
  183.0 3.3 %multiply_convert_fusion = bf16[2,2048,256]{2,1,0:T(8,128)(2,1)S(1)} fusion(f32[2,2048,256]{2,1,0:T(8,128)} %all-reduce.4.cloned.1.call-done, f32[2048,256]{1,0:T(8,128)} %broadcast_multiply_fusion), kind=kLoop, calls=%fused_computation.12 | loop fusion | flops 2097152 | bytes 8388608 | tf_op jit(solution)/shard_map/convert_element_type | solution.py:141
  186.4 1.3 copy-done.1
  187.7 6.8 %fusion.7 = f32[256,256]{1,0:T(8,128)S(1)} fusion(bf16[2,2048,256]{2,1,0:T(8,128)(2,1)S(1)} %multiply_convert_fusion, f32[2048,256]{1,0:T(8,128)S(1)} %fusion.38), kind=kOutput, calls=%fused_computation.30 | convolution fusion | flops 268959744 | bytes 3407872 | tf_op jit(solution)/shard_map/dot_general | solution.py:142
  194.5 9.1 %fusion.5 = bf16[1,1,256,256]{3,2,1,0:T(8,128)(2,1)} fusion(bf16[256,256]{1,0:T(8,128)(2,1)S(1)} %copy-done.5, f32[256,256]{1,0:T(8,128)S(1)} %fusion.7, bf16[2,2048,256]{2,1,0:T(8,128)(2,1)} %copy-done.1, f32[2048,256]{1,0:T(8,128)S(1)} %fusion.38, f32[256,256]{1,0:T(8,128)S(1)} %reduce_sum.19, bf16[1,1,256,256]{3,2,1,0:T(8,128)(2,1)S(1)} %copy-done.2), kind=kOutput, calls=%fused_computation.26 | convolution fusion | flops 302972928 | bytes 4063232 | tf_op jit(solution)/shard_map/dot_general | solution.py:147
  (73 shorter events, 6.3 us)
Async XLA Ops:
  6.5 135.9 %copy-start = (bf16[256,256]{1,0:T(8,128)(2,1)S(1)}, bf16[256,256]{1,0:T(8,128)(2,1)}, u32[]{:S(2)}) copy-start(bf16[256,256]{1,0:T(8,128)(2,1)} %param.22) | copy-start | bytes 393220
  6.5 12.0 %copy-start.2 = (bf16[1,1,256,256]{3,2,1,0:T(8,128)(2,1)S(1)}, bf16[1,1,256,256]{3,2,1,0:T(8,128)(2,1)}, u32[]{:S(2)}) copy-start(bf16[1,1,256,256]{3,2,1,0:T(8,128)(2,1)} %param.12) | copy-start | bytes 393220
  6.5 12.0 %copy-start.4 = (bf16[256,256]{1,0:T(8,128)(2,1)S(1)}, bf16[256,256]{1,0:T(8,128)(2,1)}, u32[]{:S(2)}) copy-start(bf16[256,256]{1,0:T(8,128)(2,1)} %param.19) | copy-start | bytes 393220
  6.5 176.5 %all-reduce.4.cloned.1.call-start = ((), (), s32[]{:S(2)}) async-start(), calls=%async_computation | async-start | bytes 8388608 | tf_op jit(solution)/shard_map/psum | solution.py:140
  7.3 35.3 %collective-permute-start = (bf16[1,1,3,256]{3,1,2,0:T(2,128)(2,1)S(1)}, bf16[1,1,3,256]{3,1,2,0:T(2,128)(2,1)S(1)}, u32[]{:S(2)}, u32[]{:S(2)}) collective-permute-start(bf16[1,1,3,256]{3,1,2,0:T(2,128)(2,1)S(1)} %convert_element_type.71), channel_id=1, source_target_pairs={{0,8},{8,16},{16,24},{24,0},{1,9},{9,17},{17,25},{25,1},{2,10},{10... | collective-permute-start | bytes 4616 | tf_op jit(solution)/shard_map/ppermute | solution.py:20
  10.2 32.4 %collective-permute-start.1 = (bf16[1,1,3,256]{3,1,2,0:T(2,128)(2,1)S(1)}, bf16[1,1,3,256]{3,1,2,0:T(2,128)(2,1)S(1)}, u32[]{:S(2)}, u32[]{:S(2)}) collective-permute-start(bf16[1,1,3,256]{3,1,2,0:T(2,128)(2,1)S(1)} %convert_element_type.71), channel_id=1, source_target_pairs={{8,0},{16,8},{24,16},{0,24},{9,1},{17,9},{25,17},{1,25},{10,2},{18... | collective-permute-start | bytes 4616 | tf_op jit(solution)/shard_map/ppermute | solution.py:23
  13.0 77.8 %collective-permute-start.4 = (bf16[1,1,256,256]{3,2,1,0:T(8,128)(2,1)}, bf16[1,1,256,256]{3,2,1,0:T(8,128)(2,1)}, u32[]{:S(2)}, u32[]{:S(2)}) collective-permute-start(bf16[1,1,256,256]{3,2,1,0:T(8,128)(2,1)} %fusion.6), channel_id=1, source_target_pairs={{0,8},{8,16},{16,24},{24,0},{1,9},{9,17},{17,25},{25,1},{2,10},{10... | collective-permute-start | bytes 393224 | tf_op jit(solution)/shard_map/ppermute | solution.py:20
  14.1 76.7 %collective-permute-start.5 = (bf16[1,1,256,256]{3,2,1,0:T(8,128)(2,1)}, bf16[1,1,256,256]{3,2,1,0:T(8,128)(2,1)}, u32[]{:S(2)}, u32[]{:S(2)}) collective-permute-start(bf16[1,1,256,256]{3,2,1,0:T(8,128)(2,1)} %fusion.6), channel_id=1, source_target_pairs={{8,0},{16,8},{24,16},{0,24},{9,1},{17,9},{25,17},{1,25},{10,2},{18... | collective-permute-start | bytes 393224 | tf_op jit(solution)/shard_map/ppermute | solution.py:23
  39.2 0.7 copy-start.14
  39.2 0.8 copy-start.7
  39.2 0.8 copy-start.3
  39.2 0.9 copy-start.6
  39.2 1.7 copy-start.17
  42.6 9.1 %collective-permute-start.2 = (bf16[3,1,3,256]{3,1,2,0:T(2,128)(2,1)S(1)}, bf16[3,1,3,256]{3,1,2,0:T(2,128)(2,1)S(1)}, u32[]{:S(2)}, u32[]{:S(2)}) collective-permute-start(bf16[3,1,3,256]{3,1,2,0:T(2,128)(2,1)S(1)} %pad_maximum_fusion.2), channel_id=1, source_target_pairs={{0,1},{1,2},{2,3},{3,4},{4,5},{5,6},{6,7},{7,0},{8,9},{9,10},{10,1... | collective-permute-start | bytes 13832 | tf_op jit(solution)/shard_map/ppermute | solution.py:20
  42.7 9.0 %collective-permute-start.3 = (bf16[3,1,3,256]{3,1,2,0:T(2,128)(2,1)S(1)}, bf16[3,1,3,256]{3,1,2,0:T(2,128)(2,1)S(1)}, u32[]{:S(2)}, u32[]{:S(2)}) collective-permute-start(bf16[3,1,3,256]{3,1,2,0:T(2,128)(2,1)S(1)} %pad_maximum_fusion.2), channel_id=1, source_target_pairs={{1,0},{2,1},{3,2},{4,3},{5,4},{6,5},{7,6},{0,7},{9,8},{10,9},{11,1... | collective-permute-start | bytes 13832 | tf_op jit(solution)/shard_map/ppermute | solution.py:23
  91.9 9.2 %copy-start.8 = (s32[4,2,8,128]{3,1,2,0:T(2,128)S(1)}, s32[4,2,8,128]{3,1,2,0:T(2,128)}, u32[]{:S(2)}) copy-start(s32[4,2,8,128]{3,1,2,0:T(2,128)} %copy.19) | copy-start | bytes 98308
  91.9 9.2 %copy-start.9 = (s32[4,2,8,128]{3,1,2,0:T(2,128)S(1)}, s32[4,2,8,128]{3,1,2,0:T(2,128)}, u32[]{:S(2)}) copy-start(s32[4,2,8,128]{3,1,2,0:T(2,128)} %copy.21) | copy-start | bytes 98308
  91.9 9.2 %copy-start.10 = (s32[4,2,8,128]{3,1,2,0:T(2,128)S(1)}, s32[4,2,8,128]{3,1,2,0:T(2,128)}, u32[]{:S(2)}) copy-start(s32[4,2,8,128]{3,1,2,0:T(2,128)} %copy.22) | copy-start | bytes 98308
  91.9 9.2 %copy-start.11 = (f32[4,2,8,128]{3,1,2,0:T(2,128)S(1)}, f32[4,2,8,128]{3,1,2,0:T(2,128)}, u32[]{:S(2)}) copy-start(f32[4,2,8,128]{3,1,2,0:T(2,128)} %copy.20) | copy-start | bytes 98308
  91.9 9.2 %copy-start.12 = (f32[4,2,8,128]{3,1,2,0:T(2,128)S(1)}, f32[4,2,8,128]{3,1,2,0:T(2,128)}, u32[]{:S(2)}) copy-start(f32[4,2,8,128]{3,1,2,0:T(2,128)} %copy.23) | copy-start | bytes 98308
  91.9 9.2 %copy-start.13 = (f32[4,2,8,128]{3,1,2,0:T(2,128)S(1)}, f32[4,2,8,128]{3,1,2,0:T(2,128)}, u32[]{:S(2)}) copy-start(f32[4,2,8,128]{3,1,2,0:T(2,128)} %copy.24) | copy-start | bytes 98308
  91.9 9.2 %copy-start.15 = (pred[8192]{0:T(1024)(128)(4,1)S(1)}, pred[8192]{0:T(1024)(128)(4,1)}, u32[]{:S(2)}) copy-start(pred[8192]{0:T(1024)(128)(4,1)} %ne.82) | copy-start | bytes 24580
  92.0 9.2 %copy-start.16 = (pred[8192]{0:T(1024)(128)(4,1)S(1)}, pred[8192]{0:T(1024)(128)(4,1)}, u32[]{:S(2)}) copy-start(pred[8192]{0:T(1024)(128)(4,1)} %ne.84) | copy-start | bytes 24580
  92.0 13.5 %collective-permute-start.6 = (bf16[3,1,256,256]{3,2,1,0:T(8,128)(2,1)S(1)}, bf16[3,1,256,256]{3,2,1,0:T(8,128)(2,1)S(1)}, u32[]{:S(2)}, u32[]{:S(2)}) collective-permute-start(bf16[3,1,256,256]{3,2,1,0:T(8,128)(2,1)S(1)} %pad_maximum_fusion.1), channel_id=1, source_target_pairs={{0,1},{1,2},{2,3},{3,4},{4,5},{5,6},{6,7},{7,0},{8,9},{9,10},{10,1... | collective-permute-start | bytes 1179656 | tf_op jit(solution)/shard_map/ppermute | solution.py:20
  92.0 13.4 %collective-permute-start.7 = (bf16[3,1,256,256]{3,2,1,0:T(8,128)(2,1)S(1)}, bf16[3,1,256,256]{3,2,1,0:T(8,128)(2,1)S(1)}, u32[]{:S(2)}, u32[]{:S(2)}) collective-permute-start(bf16[3,1,256,256]{3,2,1,0:T(8,128)(2,1)S(1)} %pad_maximum_fusion.1), channel_id=1, source_target_pairs={{1,0},{2,1},{3,2},{4,3},{5,4},{6,5},{7,6},{0,7},{9,8},{10,9},{11,1... | collective-permute-start | bytes 1179656 | tf_op jit(solution)/shard_map/ppermute | solution.py:23
  106.7 35.8 %copy-start.18 = (f32[256]{0:T(256)S(1)}, f32[256]{0:T(256)}, u32[]{:S(2)}) copy-start(f32[256]{0:T(256)} %param.21) | copy-start | bytes 3076
  186.4 1.3 copy-start.1
  187.7 6.8 %copy-start.5 = (bf16[256,256]{1,0:T(8,128)(2,1)S(1)}, bf16[256,256]{1,0:T(8,128)(2,1)}, u32[]{:S(2)}) copy-start(bf16[256,256]{1,0:T(8,128)(2,1)} %param.23) | copy-start | bytes 393220
Sparse Core Ops, SparseCore 0:
  39.4 143.6 all-reduce.3
where the time goes:
time: 212 us; the launch traced here: 210 us
  local copies, waits for them, and re-layouts  80.1 us (38%)
  matrix products  49 us (23%)
  waiting for transfers between devices  29.4 us (14%)
  other arithmetic  24.2 us (11%)
  starting transfers between devices  14 us (7%)
  between operations  13.8 us (7%)
    gather x1, local copies, waits for them, and re-layouts, block_messages(): gathered = jnp.take(near_table, flat_slots, axis=0)  35.7 us
    gather x1, local copies, waits for them, and re-layouts, block_messages(): jnp.take(near_coords, flat_slots, axis=1).reshape(3, slot_count, atom_count)  30.5 us
    psum x1, waiting for transfers between devices, local(): totals = lax.psum(partials, ('role', 'atoms'))  25.7 us
    dot_general x2, matrix products, contract_rows(): lax.dot_general(left_side, right_side, (((0,), (0,)), ((), ())), preferre...  18.1 us
    dot_general x1, matrix products, block_messages(): filters = jnp.dot(inner, w_filter, preferred_element_type=jnp.float32)  10.3 us
    ppermute x4, starting transfers between devices, padded(): lax.ppermute(lax.slice_in_dim(block, 0, width, axis=dim), axis, backward)  9.88 us
    dot_general x1, matrix products, local(): jnp.dot(combined, w_out, preferred_element_type=jnp.float32)  9.13 us
    dot_general x1, matrix products, local(): jnp.dot(cosine, filtered[0], preferred_element_type=jnp.float32)  6.79 us
  transfers between devices with their start and end apart: 9, of which 2 were waited for; matrix products, arithmetic and copies ran while one was open for 62% of the time, Pallas kernels for 0%

commit v1 on v0

v1 whole, which is shorter than its diff:
```python
import functools
import math

import jax
import jax.numpy as jnp
from jax import lax
from jax.experimental import pallas as pl
from jax.experimental.pallas import tpu as pltpu
from jax.sharding import PartitionSpec as P

soft_sq = 0.01
damping = 64.0
ewald_scale = 0.25
coord_rows = 16
piece_rows = 16
MESH = pl.DeviceIdType.MESH


def contract_first(left, right):
    return lax.dot_general(
        left, right, (((0,), (0,)), ((), ())), preferred_element_type=jnp.float32
    )


def dot(left, right):
    return jnp.dot(left, right, preferred_element_type=jnp.float32)


def flipped(array):
    return jnp.transpose(array.astype(jnp.float32))


def turns_cos_sin(turns):
    r = turns - jnp.floor(turns + 0.5)
    u = r * r
    sin_half = jnp.full_like(u, -(math.pi**11) / math.factorial(11))
    for power in (9, 7, 5, 3, 1):
        sign = 1.0 if power % 4 == 1 else -1.0
        sin_half = sin_half * u + sign * math.pi**power / math.factorial(power)
    sin_half = sin_half * r
    cos_half = jnp.full_like(u, math.pi**12 / math.factorial(12))
    for power in (10, 8, 6, 4, 2, 0):
        sign = 1.0 if power % 4 == 0 else -1.0
        cos_half = cos_half * u + sign * math.pi**power / math.factorial(power)
    return 1.0 - 2.0 * sin_half * sin_half, 2.0 * sin_half * cos_half


def exchange_plan(role_count, atoms_count, rows):
    role, atoms = lax.axis_index("role"), lax.axis_index("atoms")
    core = atoms % 2
    role_bits = role_count.bit_length() - 1
    atom_bits = atoms_count.bit_length() - 1
    partners = [(core, (role, atoms + 1 - 2 * core))]
    for stage in range(role_bits):
        if role_bits == 2:
            which = (stage + core) % 2
            low, high = role % 2, (role // 2) % 2
            bit = low + which * (high - low)
            partners.append((bit, (role + (1 - 2 * bit) * (1 + which), atoms)))
        else:
            bit = (role // 2**stage) % 2
            partners.append((bit, (role + (1 - 2 * bit) * 2**stage, atoms)))
    for stage in range(1, atom_bits):
        bit = (atoms // 2**stage) % 2
        partners.append((bit, (role, atoms + (1 - 2 * bit) * 2**stage)))
    plan = []
    start, length = 0, rows
    for bit, device in partners:
        length //= 2
        keep = start + bit * length
        send = start + (1 - bit) * length
        plan.append((device, keep, send, length))
        start = keep
    return plan


def block_kernel(
    role_count,
    atoms_count,
    features,
    positions,
    neighbours,
    images,
    waves,
    kgain,
    w_in,
    w_query,
    w_rbf,
    b_rbf,
    w_filter,
    w_out,
    result,
    table,
    pieces,
    phase,
    phase_t,
    sums,
    staged,
    landed,
    filtered,
    gain,
    offsets,
    blocks,
    wide_a,
    wide_b,
    messages,
    rbf_t,
    filter_t,
    bias,
    halo_send,
    halo_recv,
    cut_send,
    cut_recv,
    join_send,
    join_recv,
):
    role, atoms = lax.axis_index("role"), lax.axis_index("atoms")
    atom_count, width = features.shape
    slot_count = neighbours.shape[0]
    wave_count = waves.shape[0]
    basis_count = w_rbf.shape[0]
    rows = 2 * wave_count
    plan = exchange_plan(role_count, atoms_count, rows)
    around = []
    for da in (-1, 0, 1):
        for db in (-1, 0, 1):
            if da or db:
                device = (
                    (role + da + role_count) % role_count,
                    (atoms + db + atoms_count) % atoms_count,
                )
                around.append((device, (1 - da) * 3 + (1 - db)))

    barrier = pltpu.get_barrier_semaphore()
    for device, _ in around:
        pl.semaphore_signal(barrier, inc=1, device_id=device, device_id_type=MESH)
    for device, _, _, _ in plan:
        pl.semaphore_signal(barrier, inc=1, device_id=device, device_id_type=MESH)

    own = positions[...]
    high = own.astype(jnp.bfloat16).astype(jnp.float32)
    rest = own - high
    middle = rest.astype(jnp.bfloat16).astype(jnp.float32)
    pieces[...] = jnp.zeros_like(pieces)
    pieces[0:3, :] = high
    pieces[3:6, :] = middle
    pieces[6:9, :] = rest - middle
    pos_pieces = pieces[...].astype(jnp.bfloat16)
    hidden = dot(features[...], w_in[...]).astype(jnp.bfloat16)
    table[4, 0:width, :] = flipped(hidden).astype(jnp.bfloat16)
    table[4, width : width + coord_rows, :] = pos_pieces

    pl.semaphore_wait(barrier, len(around) + len(plan))
    halo = []
    for number, (device, slot) in enumerate(around):
        copy = pltpu.make_async_remote_copy(
            src_ref=table.at[4],
            dst_ref=table.at[slot],
            send_sem=halo_send.at[number],
            recv_sem=halo_recv.at[number],
            device_id=device,
            device_id_type=MESH,
        )
        copy.start()
        halo.append(copy)

    queries = dot(features[...], w_query[...]).astype(jnp.bfloat16)
    chunk = 256

    @pl.loop(0, wave_count // chunk)
    def _(step):
        first = pl.multiple_of(step * chunk, chunk)
        turns = dot(waves[pl.ds(first, chunk), :], pos_pieces)
        cosine, sine = turns_cos_sin(turns)
        cosine, sine = cosine.astype(jnp.bfloat16), sine.astype(jnp.bfloat16)
        phase[pl.ds(first, chunk), :] = cosine
        phase[pl.ds(wave_count + first, chunk), :] = sine
        sums[pl.ds(first, chunk), :] = dot(cosine, queries)
        sums[pl.ds(wave_count + first, chunk), :] = dot(sine, queries)

    def cut(stage):
        device, _, send, length = plan[stage]
        place = rows - 2 * length
        staged[pl.ds(place, length), :] = sums[
            pl.ds(pl.multiple_of(send, piece_rows), length), :
        ].astype(jnp.bfloat16)
        copy = pltpu.make_async_remote_copy(
            src_ref=staged.at[pl.ds(place, length)],
            dst_ref=landed.at[pl.ds(place, length)],
            send_sem=cut_send.at[stage],
            recv_sem=cut_recv.at[stage],
            device_id=device,
            device_id_type=MESH,
        )
        copy.start()
        return copy

    def add_cut(stage):
        _, keep, _, length = plan[stage]
        place = rows - 2 * length
        where = pl.ds(pl.multiple_of(keep, piece_rows), length)
        sums[where, :] = sums[where, :] + landed[pl.ds(place, length), :].astype(jnp.float32)

    def join(stage):
        device, keep, _, length = plan[stage]
        where = pl.ds(pl.multiple_of(keep, piece_rows), length)
        copy = pltpu.make_async_remote_copy(
            src_ref=filtered.at[where],
            dst_ref=filtered.at[where],
            send_sem=join_send.at[stage],
            recv_sem=join_recv.at[stage],
            device_id=device,
            device_id_type=MESH,
        )
        copy.start()
        return copy

    in_flight = cut(0)

    rbf_t[...] = flipped(w_rbf[...]).astype(jnp.bfloat16)
    filter_t[...] = flipped(w_filter[...]).astype(jnp.bfloat16)
    bias[...] = jnp.transpose(jnp.broadcast_to(b_rbf[...], (atom_count, width)))
    entry = neighbours[...]
    brick = entry // atom_count
    blocks[0] = brick.astype(jnp.float32)
    blocks[1] = (entry - brick * atom_count).astype(jnp.float32)
    image = images[...]
    first_part = jnp.where(image >= 9, 1, 0) + jnp.where(image >= 18, 1, 0)
    left = image - 9 * first_part
    second_part = jnp.where(left >= 3, 1, 0) + jnp.where(left >= 6, 1, 0)
    third_part = left - 3 * second_part
    for axis, part in enumerate((first_part, second_part, third_part)):
        offsets[axis] = (part - 1).astype(jnp.float32) - own[axis : axis + 1, :]
    messages[...] = jnp.zeros_like(messages)

    wave_part = waves[...]
    picks = jnp.where(
        lax.broadcasted_iota(jnp.int32, (waves.shape[1], 128), 0) < 3, 1.0, 0.0
    ).astype(jnp.bfloat16)
    squares = dot(wave_part * wave_part, picks)
    gain[...] = jnp.exp(squares * (-1.0 / damping)) / squares

    @pl.loop(0, rows // chunk)
    def _(step):
        first = pl.multiple_of(step * chunk, chunk)
        phase_t[:, pl.ds(first, chunk)] = flipped(phase[pl.ds(first, chunk), :]).astype(
            jnp.bfloat16
        )

    lane_atoms = lax.broadcasted_iota(jnp.int32, (atom_count, atom_count), 0).astype(
        jnp.float32
    ).astype(jnp.bfloat16)
    centers = lax.broadcasted_iota(jnp.int32, (basis_count, atom_count), 0).astype(
        jnp.float32
    ) * (4.0 / (basis_count - 1))
    sharpness = (basis_count / 4.0) ** 2
    one, zero = jnp.ones((), jnp.bfloat16), jnp.zeros((), jnp.bfloat16)

    def gather(slot, target):
        brick_row = blocks[0, pl.ds(slot, 1), :]
        atom_row = blocks[1, pl.ds(slot, 1), :]
        total = jnp.zeros((width + coord_rows, atom_count), jnp.float32)
        for number in range(9):
            wanted = jnp.where(brick_row == float(number), atom_row, -1.0).astype(jnp.bfloat16)
            chosen = jnp.where(lane_atoms == wanted, one, zero)
            total += dot(table[number], chosen)
        target[...] = total

    def filter_slot(slot, source):
        square = jnp.full((1, atom_count), soft_sq, jnp.float32)
        for axis in range(3):
            near = (
                source[width + axis : width + axis + 1, :]
                + source[width + 3 + axis : width + 4 + axis, :]
                + source[width + 6 + axis : width + 7 + axis, :]
            )
            delta = near + offsets[axis, pl.ds(slot, 1), :]
            square += delta * delta
        away = jnp.sqrt(square) - centers
        basis = jnp.exp(-sharpness * (away * away)).astype(jnp.bfloat16)
        before = dot(rbf_t[...], basis) + bias[...]
        inner = (
            jnp.maximum(before, 0.0)
            + jnp.log(1.0 + jnp.exp(-jnp.abs(before)))
            - math.log(2.0)
        ).astype(jnp.bfloat16)
        messages[...] += dot(filter_t[...], inner) * source[0:width, :]

    pairs = slot_count // 2

    def short_range(first, last):
        if last <= first:
            return

        @pl.loop(first, last)
        def _(pair):
            slot = pair * 2
            gather(slot + 1, wide_b)
            filter_slot(slot, wide_a)
            gather(lax.rem(slot + 2, slot_count), wide_a)
            filter_slot(slot + 1, wide_b)

    for copy in halo:
        copy.wait()
    gather(0, wide_a)

    stages = len(plan)
    share = [pairs * step // (2 * stages - 1) for step in range(2 * stages)]
    for stage in range(stages):
        if stage:
            short_range(share[stage - 1], share[stage])
        in_flight.wait()
        add_cut(stage)
        if stage + 1 < stages:
            in_flight = cut(stage + 1)

    _, mine, _, mine_rows = plan[-1]
    scale = (atom_count * role_count * atoms_count) ** (-0.5) * ewald_scale
    channel = kgain[...] * scale
    where = pl.ds(pl.multiple_of(mine, piece_rows), mine_rows)
    gain_rows = gain[pl.ds(pl.multiple_of(mine % wave_count, piece_rows), mine_rows), :]
    for part in range(width // 128):
        lanes = pl.ds(part * 128, 128)
        filtered[where, lanes] = (
            sums[where, lanes] * gain_rows * channel[:, part * 128 : part * 128 + 128]
        ).astype(jnp.bfloat16)

    for number, stage in enumerate(reversed(range(stages))):
        in_flight = join(stage)
        short_range(share[stages - 1 + number], share[stages + number])
        if number == stages - 1:
            short = jnp.transpose(messages[...]) * slot_count ** (-0.5)
        in_flight.wait()

    combined = (short + dot(phase_t[...], filtered[...])).astype(jnp.bfloat16)
    result[...] = (features[...].astype(jnp.float32) + dot(combined, w_out[...])).astype(
        jnp.bfloat16
    )


def local(
    role_count,
    atoms_count,
    features,
    positions,
    neighbours,
    images,
    wave,
    kgain,
    w_in,
    w_query,
    w_rbf,
    b_rbf,
    w_filter,
    w_out,
):
    own_rows = features[0, 0]
    atom_count, width = own_rows.shape
    wave_count = wave.shape[1]
    slot_count = neighbours.shape[2]
    rows = 2 * wave_count
    stages = (role_count * atoms_count).bit_length() - 1
    waves = jnp.transpose(
        jnp.pad(jnp.concatenate([wave] * 3, axis=0), ((0, piece_rows - 9), (0, 0)))
    ).astype(jnp.bfloat16)
    vmem = pl.BlockSpec(memory_space=pltpu.VMEM)
    full = width + coord_rows
    out = pl.pallas_call(
        functools.partial(block_kernel, role_count, atoms_count),
        out_shape=jax.ShapeDtypeStruct((atom_count, width), jnp.bfloat16),
        in_specs=[vmem] * 12,
        out_specs=vmem,
        scratch_shapes=[
            pltpu.VMEM((9, full, atom_count), jnp.bfloat16),
            pltpu.VMEM((piece_rows, atom_count), jnp.float32),
            pltpu.VMEM((rows, atom_count), jnp.bfloat16),
            pltpu.VMEM((atom_count, rows), jnp.bfloat16),
            pltpu.VMEM((rows, width), jnp.float32),
            pltpu.VMEM((rows, width), jnp.bfloat16),
            pltpu.VMEM((rows, width), jnp.bfloat16),
            pltpu.VMEM((rows, width), jnp.bfloat16),
            pltpu.VMEM((wave_count, 128), jnp.float32),
            pltpu.VMEM((3, slot_count, atom_count), jnp.float32),
            pltpu.VMEM((2, slot_count, atom_count), jnp.float32),
            pltpu.VMEM((full, atom_count), jnp.float32),
            pltpu.VMEM((full, atom_count), jnp.float32),
            pltpu.VMEM((width, atom_count), jnp.float32),
            pltpu.VMEM((width, w_rbf.shape[0]), jnp.bfloat16),
            pltpu.VMEM((width, width), jnp.bfloat16),
            pltpu.VMEM((width, atom_count), jnp.float32),
            pltpu.SemaphoreType.DMA((8,)),
            pltpu.SemaphoreType.DMA((8,)),
            pltpu.SemaphoreType.DMA((stages,)),
            pltpu.SemaphoreType.DMA((stages,)),
            pltpu.SemaphoreType.DMA((stages,)),
            pltpu.SemaphoreType.DMA((stages,)),
        ],
        compiler_params=pltpu.CompilerParams(
            collective_id=0, has_side_effects=True, vmem_limit_bytes=48 * 1024 * 1024
        ),
    )(
        own_rows,
        positions[0, 0],
        neighbours[0, 0],
        images[0, 0],
        waves,
        kgain[None, :],
        w_in,
        w_query,
        w_rbf,
        b_rbf[None, :],
        w_filter,
        w_out,
    )
    return out[None, None]


def solution(mesh):
    placed = P("role", "atoms", None, None)
    body = functools.partial(local, mesh.shape["role"], mesh.shape["atoms"])
    return jax.shard_map(
        body,
        mesh=mesh,
        in_specs=(placed,) * 4 + (P(),) * 8,
        out_specs=placed,
        check_vma=False,
    )
```

time: 212 us -> 78.5 us (0.37)
  local copies, waits for them, and re-layouts: 80.1 us -> 2.31 us
  Pallas kernels: 0 us -> 75.1 us
  matrix products: 49 us -> 0 us
  waiting for transfers between devices: 29.4 us -> 0 us
  other arithmetic: 24.2 us -> 0.8 us
  starting transfers between devices: 14 us -> 0 us
  between operations: 13.8 us -> 0.11 us
    pallas_call x0 -> x1, Pallas kernels: none -> 75.1 us  [local(): pl.pallas_call(functools.partial(block_kernel, role_count, atoms_count),...]
    gather x2 -> x0, local copies, waits for them, and re-layouts: 66.3 us -> none  [the longest x1 35.7 us: block_messages(): gathered = jnp.take(near_table, flat_slots, axis=0)]
    dot_general x8 -> x0, matrix products: 49 us -> none  [the longest x2 18.1 us: contract_rows(): lax.dot_general(left_side, right_side, (((0,), (0,)), ((), ())), preferre...]
    psum x1 -> x0, waiting for transfers between devices: 25.7 us -> none  [local(): totals = lax.psum(partials, ('role', 'atoms'))]
    ppermute x8 -> x0, starting transfers between devices: 14 us -> none  [the longest x4 9.88 us: padded(): lax.ppermute(lax.slice_in_dim(block, 0, width, axis=dim), axis, backward)]
    select_n x2 -> x0, other arithmetic: 6.28 us -> none  [block_messages(): jnp.take(near_coords, flat_slots, axis=1).reshape(3, slot_count, atom_count)]
    slice x2 -> x0, local copies, waits for them, and re-layouts: 5.48 us -> none  [the longest x1 5.48 us: block_messages(): near_pos[2] + (near_images % 3 - 1).astype(jnp.float32) * box_side]
    reduce_sum x2 -> x0, other arithmetic: 4.52 us -> none  [the longest x1 4.5 us: block_messages(): return (filters * gathered).reshape(slot_count, atom_count, -1).sum(axis=0)]
  transfers between devices with their start and end apart: 9 -> 0, of which waited for: 2 -> 0; matrix products, arithmetic and copies ran while one was open for 62% -> 0% of each run, Pallas kernels for 0% -> 0%
where the time goes in v1:
time: 78.5 us; the launch traced here: 78.3 us
  Pallas kernels  75.1 us (96%)
  local copies, waits for them, and re-layouts  2.31 us (3%)
  other arithmetic  0.8 us (1%)
    pallas_call x1, Pallas kernels, local(): pl.pallas_call(functools.partial(block_kernel, role_count, atoms_count),...  75.1 us
    unnamed x24, local copies, waits for them, and re-layouts  1.91 us

profile of v1, /device:TPU:0, one launch (start us, length us, event | category | flops | bytes accessed | tf_op | source)
XLA Modules:
  0.0 78.3 jit_solution(17798157999574188771)
XLA Ops:
  0.0 0.8 convert.7
  0.8 0.3 copy.16
  1.1 0.0 copy-start.10
  1.1 0.0 copy-start
  1.1 0.0 copy-start.1
  1.1 0.0 copy-start.2
  1.2 0.0 copy-start.3
  1.2 0.0 copy-start.4
  1.2 0.0 copy-start.5
  1.2 0.0 copy-start.6
  1.2 0.0 copy-start.7
  1.2 0.0 copy-start.9
  1.2 0.1 pad_bitcast_fusion.waves
  1.3 0.5 copy-done.10
  1.8 0.0 copy-start.8
  1.8 0.2 copy-done
  2.0 0.1 copy-done.1
  2.1 0.1 copy-done.2
  2.2 0.1 copy-done.3
  2.2 0.1 copy-done.4
  2.3 0.0 copy-done.5
  2.3 0.0 copy-done.6
  2.3 0.0 copy-done.7
  2.3 0.0 copy-done.9
  2.3 0.2 copy-done.8
  2.6 75.1 %shard_map.118 = bf16[256,256]{1,0:T(8,128)(2,1)S(1)} custom-call(bf16[256,256]{1,0:T(8,128)(2,1)S(1)} %bitcast.12, f32[3,256]{1,0:T(4,128)S(1)} %bitcast.15, s32[32,256]{1,0:T(8,128)S(1)} %bitcast.13, s32[32,256]{1,0:T(8,128)S(1)} %bitcast.14, bf16[2048,16]{1,0:T(8,128)(2,1)S(1)} %pad_bitcast_fusion.waves, f32[1,256]{1,0:T(1,128)S(1)} %bitcast.16, ...), custom_call_target="tpu_custom_call" | custom-call | tf_op jit(solution)/shard_map/pallas_call | solution.py:368
  77.6 0.7 copy.21
  (2 shorter events, 0.0 us)
Async XLA Ops:
  1.1 0.7 copy-start.10
  1.1 0.9 %copy-start = (bf16[1,1,256,256]{3,2,1,0:T(8,128)(2,1)S(1)}, bf16[1,1,256,256]{3,2,1,0:T(8,128)(2,1)}, u32[]{:S(2)}) copy-start(bf16[1,1,256,256]{3,2,1,0:T(8,128)(2,1)} %param.12) | copy-start | bytes 393220
  1.1 1.0 %copy-start.1 = (bf16[256,256]{1,0:T(8,128)(2,1)S(1)}, bf16[256,256]{1,0:T(8,128)(2,1)}, u32[]{:S(2)}) copy-start(bf16[256,256]{1,0:T(8,128)(2,1)} %w_in.1) | copy-start | bytes 393220
  1.1 1.0 %copy-start.2 = (bf16[256,256]{1,0:T(8,128)(2,1)S(1)}, bf16[256,256]{1,0:T(8,128)(2,1)}, u32[]{:S(2)}) copy-start(bf16[256,256]{1,0:T(8,128)(2,1)} %w_query.1) | copy-start | bytes 393220
  1.2 1.1 %copy-start.3 = (bf16[256,256]{1,0:T(8,128)(2,1)S(1)}, bf16[256,256]{1,0:T(8,128)(2,1)}, u32[]{:S(2)}) copy-start(bf16[256,256]{1,0:T(8,128)(2,1)} %w_filter.1) | copy-start | bytes 393220
  1.2 1.1 %copy-start.4 = (bf16[256,256]{1,0:T(8,128)(2,1)S(1)}, bf16[256,256]{1,0:T(8,128)(2,1)}, u32[]{:S(2)}) copy-start(bf16[256,256]{1,0:T(8,128)(2,1)} %w_out.1) | copy-start | bytes 393220
  1.2 1.1 %copy-start.5 = (s32[1,1,32,256]{3,2,1,0:T(8,128)S(1)}, s32[1,1,32,256]{3,2,1,0:T(8,128)}, u32[]{:S(2)}) copy-start(s32[1,1,32,256]{3,2,1,0:T(8,128)} %param.14) | copy-start | bytes 98308
  1.2 1.1 %copy-start.6 = (s32[1,1,32,256]{3,2,1,0:T(8,128)S(1)}, s32[1,1,32,256]{3,2,1,0:T(8,128)}, u32[]{:S(2)}) copy-start(s32[1,1,32,256]{3,2,1,0:T(8,128)} %param.15) | copy-start | bytes 98308
  1.2 1.1 %copy-start.7 = (bf16[64,256]{1,0:T(8,128)(2,1)S(1)}, bf16[64,256]{1,0:T(8,128)(2,1)}, u32[]{:S(2)}) copy-start(bf16[64,256]{1,0:T(8,128)(2,1)} %w_rbf.1) | copy-start | bytes 98308
  1.2 1.1 %copy-start.9 = (f32[256]{0:T(256)S(1)}, f32[256]{0:T(256)}, u32[]{:S(2)}) copy-start(f32[256]{0:T(256)} %param.21) | copy-start | bytes 3076
  1.8 0.8 copy-start.8

commit v2 on v1

--- a/solution.py
+++ b/solution.py
@@ -121,18 +121,16 @@
     basis_count = w_rbf.shape[0]
     rows = 2 * wave_count
     plan = exchange_plan(role_count, atoms_count, rows)
-    around = []
-    for da in (-1, 0, 1):
-        for db in (-1, 0, 1):
-            if da or db:
-                device = (
-                    (role + da + role_count) % role_count,
-                    (atoms + db + atoms_count) % atoms_count,
-                )
-                around.append((device, (1 - da) * 3 + (1 - db)))
+    beside, along = [], []
+    for step in (-1, 1):
+        device = ((role + step + role_count) % role_count, atoms)
+        beside.append((device, 1, 1 - step, 1))
+        device = (role, (atoms + step + atoms_count) % atoms_count)
+        along.extend((device, p, p, 1 - step) for p in (1, 0, 2))
 
     barrier = pltpu.get_barrier_semaphore()
-    for device, _ in around:
+    greeted = [beside[0][0], beside[1][0], along[0][0], along[3][0]]
+    for device in greeted:
         pl.semaphore_signal(barrier, inc=1, device_id=device, device_id_type=MESH)
     for device, _, _, _ in plan:
         pl.semaphore_signal(barrier, inc=1, device_id=device, device_id_type=MESH)
@@ -150,19 +148,21 @@
     table[4, 0:width, :] = flipped(hidden).astype(jnp.bfloat16)
     table[4, width : width + coord_rows, :] = pos_pieces
 
-    pl.semaphore_wait(barrier, len(around) + len(plan))
-    halo = []
-    for number, (device, slot) in enumerate(around):
+    pl.semaphore_wait(barrier, len(greeted) + len(plan))
+
+    def send_brick(number, device, p, to_p, to_q):
         copy = pltpu.make_async_remote_copy(
-            src_ref=table.at[4],
-            dst_ref=table.at[slot],
+            src_ref=table.at[p * 3 + 1],
+            dst_ref=table.at[to_p * 3 + to_q],
             send_sem=halo_send.at[number],
             recv_sem=halo_recv.at[number],
             device_id=device,
             device_id_type=MESH,
         )
         copy.start()
-        halo.append(copy)
+        return copy
+
+    halo = [send_brick(number, *move) for number, move in enumerate(beside)]
 
     queries = dot(features[...], w_query[...]).astype(jnp.bfloat16)
     chunk = 256
@@ -216,6 +216,9 @@
         return copy
 
     in_flight = cut(0)
+    for copy in halo:
+        copy.wait()
+    halo = [send_brick(2 + number, *move) for number, move in enumerate(along)]
 
     rbf_t[...] = flipped(w_rbf[...]).astype(jnp.bfloat16)
     filter_t[...] = flipped(w_filter[...]).astype(jnp.bfloat16)
@@ -240,6 +243,10 @@
     squares = dot(wave_part * wave_part, picks)
     gain[...] = jnp.exp(squares * (-1.0 / damping)) / squares
 
+    in_flight.wait()
+    add_cut(0)
+    in_flight = cut(1)
+
     @pl.loop(0, rows // chunk)
     def _(step):
         first = pl.multiple_of(step * chunk, chunk)
@@ -259,12 +266,12 @@
     def gather(slot, target):
         brick_row = blocks[0, pl.ds(slot, 1), :]
         atom_row = blocks[1, pl.ds(slot, 1), :]
-        total = jnp.zeros((width + coord_rows, atom_count), jnp.float32)
+        chosen = []
         for number in range(9):
             wanted = jnp.where(brick_row == float(number), atom_row, -1.0).astype(jnp.bfloat16)
-            chosen = jnp.where(lane_atoms == wanted, one, zero)
-            total += dot(table[number], chosen)
-        target[...] = total
+            chosen.append(jnp.where(lane_atoms == wanted, one, zero))
+        bricks = jnp.concatenate([table[number] for number in range(9)], axis=1)
+        target[...] = dot(bricks, jnp.concatenate(chosen, axis=0))
 
     def filter_slot(slot, source):
         square = jnp.full((1, atom_count), soft_sq, jnp.float32)
@@ -300,15 +307,16 @@
             gather(lax.rem(slot + 2, slot_count), wide_a)
             filter_slot(slot + 1, wide_b)
 
-    for copy in halo:
-        copy.wait()
-    gather(0, wide_a)
-
     stages = len(plan)
-    share = [pairs * step // (2 * stages - 1) for step in range(2 * stages)]
-    for stage in range(stages):
-        if stage:
-            short_range(share[stage - 1], share[stage])
+    windows = 2 * stages - 2
+    share = [pairs * step // windows for step in range(windows + 1)]
+    for stage in range(1, stages):
+        if stage == 2:
+            for copy in halo:
+                copy.wait()
+            gather(0, wide_a)
+        if stage > 1:
+            short_range(share[stage - 2], share[stage - 1])
         in_flight.wait()
         add_cut(stage)
         if stage + 1 < stages:
@@ -327,7 +335,7 @@
 
     for number, stage in enumerate(reversed(range(stages))):
         in_flight = join(stage)
-        short_range(share[stages - 1 + number], share[stages + number])
+        short_range(share[stages - 2 + number], share[stages - 1 + number])
         if number == stages - 1:
             short = jnp.transpose(messages[...]) * slot_count ** (-0.5)
         in_flight.wait()

time: 78.5 us -> 69.9 us (0.89)
  Pallas kernels: 75.1 us -> 66.4 us
    pallas_call x1, Pallas kernels: 75.1 us -> 66.4 us  [local(): pl.pallas_call(functools.partial(block_kernel, role_count, atoms_count),...]
where the time goes in v2:
time: 69.9 us; the launch traced here: 69.7 us
  Pallas kernels  66.4 us (95%)
  local copies, waits for them, and re-layouts  2.31 us (3%)
  other arithmetic  0.8 us (1%)
    pallas_call x1, Pallas kernels, local(): pl.pallas_call(functools.partial(block_kernel, role_count, atoms_count),...  66.4 us
    unnamed x24, local copies, waits for them, and re-layouts  1.91 us

profile of v2, /device:TPU:0, one launch (start us, length us, event | category | flops | bytes accessed | tf_op | source)
XLA Modules:
  0.0 69.7 jit_solution(9661881676519679507)
XLA Ops:
  0.0 0.8 %convert.7 = bf16[3,2048]{1,0:T(4,128)(2,1)S(1)} convert(s32[3,2048]{1,0:T(4,128)} %param.16) | non-fusion elementwise | flops 6144 | bytes 36864 | tf_op jit(solution)/shard_map/convert.2
  0.8 0.3 copy.16
  1.1 0.0 copy-start.10
  1.1 0.0 copy-start
  1.1 0.0 copy-start.1
  1.1 0.0 copy-start.2
  1.2 0.0 copy-start.3
  1.2 0.0 copy-start.4
  1.2 0.0 copy-start.5
  1.2 0.0 copy-start.6
  1.2 0.0 copy-start.7
  1.2 0.0 copy-start.9
  1.2 0.1 pad_bitcast_fusion.waves
  1.3 0.5 copy-done.10
  1.8 0.0 copy-start.8
  1.8 0.2 copy-done
  2.0 0.1 copy-done.1
  2.1 0.1 copy-done.2
  2.2 0.1 copy-done.3
  2.2 0.1 copy-done.4
  2.3 0.0 copy-done.5
  2.3 0.0 copy-done.6
  2.3 0.0 copy-done.7
  2.3 0.0 copy-done.9
  2.3 0.2 copy-done.8
  2.6 66.4 %shard_map.118 = bf16[256,256]{1,0:T(8,128)(2,1)S(1)} custom-call(bf16[256,256]{1,0:T(8,128)(2,1)S(1)} %bitcast.12, f32[3,256]{1,0:T(4,128)S(1)} %bitcast.15, s32[32,256]{1,0:T(8,128)S(1)} %bitcast.13, s32[32,256]{1,0:T(8,128)S(1)} %bitcast.14, bf16[2048,16]{1,0:T(8,128)(2,1)S(1)} %pad_bitcast_fusion.waves, f32[1,256]{1,0:T(1,128)S(1)} %bitcast.16, ...), custom_call_target="tpu_custom_call" | custom-call | tf_op jit(solution)/shard_map/pallas_call | solution.py:376
  69.0 0.7 copy.21
  (2 shorter events, 0.0 us)
Async XLA Ops:
  1.1 0.7 copy-start.10
  1.1 0.9 %copy-start = (bf16[1,1,256,256]{3,2,1,0:T(8,128)(2,1)S(1)}, bf16[1,1,256,256]{3,2,1,0:T(8,128)(2,1)}, u32[]{:S(2)}) copy-start(bf16[1,1,256,256]{3,2,1,0:T(8,128)(2,1)} %param.12) | copy-start | bytes 393220
  1.1 1.0 %copy-start.1 = (bf16[256,256]{1,0:T(8,128)(2,1)S(1)}, bf16[256,256]{1,0:T(8,128)(2,1)}, u32[]{:S(2)}) copy-start(bf16[256,256]{1,0:T(8,128)(2,1)} %w_in.1) | copy-start | bytes 393220
  1.1 1.0 %copy-start.2 = (bf16[256,256]{1,0:T(8,128)(2,1)S(1)}, bf16[256,256]{1,0:T(8,128)(2,1)}, u32[]{:S(2)}) copy-start(bf16[256,256]{1,0:T(8,128)(2,1)} %w_query.1) | copy-start | bytes 393220
  1.2 1.1 %copy-start.3 = (bf16[256,256]{1,0:T(8,128)(2,1)S(1)}, bf16[256,256]{1,0:T(8,128)(2,1)}, u32[]{:S(2)}) copy-start(bf16[256,256]{1,0:T(8,128)(2,1)} %w_filter.1) | copy-start | bytes 393220
  1.2 1.1 %copy-start.4 = (bf16[256,256]{1,0:T(8,128)(2,1)S(1)}, bf16[256,256]{1,0:T(8,128)(2,1)}, u32[]{:S(2)}) copy-start(bf16[256,256]{1,0:T(8,128)(2,1)} %w_out.1) | copy-start | bytes 393220
  1.2 1.1 %copy-start.5 = (s32[1,1,32,256]{3,2,1,0:T(8,128)S(1)}, s32[1,1,32,256]{3,2,1,0:T(8,128)}, u32[]{:S(2)}) copy-start(s32[1,1,32,256]{3,2,1,0:T(8,128)} %param.14) | copy-start | bytes 98308
  1.2 1.1 %copy-start.6 = (s32[1,1,32,256]{3,2,1,0:T(8,128)S(1)}, s32[1,1,32,256]{3,2,1,0:T(8,128)}, u32[]{:S(2)}) copy-start(s32[1,1,32,256]{3,2,1,0:T(8,128)} %param.15) | copy-start | bytes 98308
  1.2 1.1 %copy-start.7 = (bf16[64,256]{1,0:T(8,128)(2,1)S(1)}, bf16[64,256]{1,0:T(8,128)(2,1)}, u32[]{:S(2)}) copy-start(bf16[64,256]{1,0:T(8,128)(2,1)} %w_rbf.1) | copy-start | bytes 98308
  1.2 1.1 %copy-start.9 = (f32[256]{0:T(256)S(1)}, f32[256]{0:T(256)}, u32[]{:S(2)}) copy-start(f32[256]{0:T(256)} %param.21) | copy-start | bytes 3076
  1.8 0.8 %copy-start.8 = (f32[256]{0:T(256)S(1)}, f32[256]{0:T(256)}, u32[]{:S(2)}) copy-start(f32[256]{0:T(256)} %param.17) | copy-start | bytes 3076

commit v3 on v2

--- a/solution.py
+++ b/solution.py
@@ -45,7 +45,7 @@
     return 1.0 - 2.0 * sin_half * sin_half, 2.0 * sin_half * cos_half
 
 
-def exchange_plan(role_count, atoms_count, rows):
+def exchange_plan(role_count, atoms_count, start, rows):
     role, atoms = lax.axis_index("role"), lax.axis_index("atoms")
     core = atoms % 2
     role_bits = role_count.bit_length() - 1
@@ -64,7 +64,7 @@
         bit = (atoms // 2**stage) % 2
         partners.append((bit, (role, atoms + (1 - 2 * bit) * 2**stage)))
     plan = []
-    start, length = 0, rows
+    length = rows
     for bit, device in partners:
         length //= 2
         keep = start + bit * length
@@ -120,7 +120,15 @@
     wave_count = waves.shape[0]
     basis_count = w_rbf.shape[0]
     rows = 2 * wave_count
-    plan = exchange_plan(role_count, atoms_count, rows)
+    chains = 2 if rows // (role_count * atoms_count) >= 2 * piece_rows else 1
+    chain_rows = rows // chains
+    chain_waves = wave_count // chains
+    plans = [
+        exchange_plan(role_count, atoms_count, chain * chain_rows, chain_rows)
+        for chain in range(chains)
+    ]
+    plan = plans[0]
+    stages = len(plan)
     beside, along = [], []
     for step in (-1, 1):
         device = ((role + step + role_count) % role_count, atoms)
@@ -167,58 +175,77 @@
     queries = dot(features[...], w_query[...]).astype(jnp.bfloat16)
     chunk = 256
 
-    @pl.loop(0, wave_count // chunk)
-    def _(step):
-        first = pl.multiple_of(step * chunk, chunk)
-        turns = dot(waves[pl.ds(first, chunk), :], pos_pieces)
-        cosine, sine = turns_cos_sin(turns)
-        cosine, sine = cosine.astype(jnp.bfloat16), sine.astype(jnp.bfloat16)
-        phase[pl.ds(first, chunk), :] = cosine
-        phase[pl.ds(wave_count + first, chunk), :] = sine
-        sums[pl.ds(first, chunk), :] = dot(cosine, queries)
-        sums[pl.ds(wave_count + first, chunk), :] = dot(sine, queries)
-
-    def cut(stage):
-        device, _, send, length = plan[stage]
-        place = rows - 2 * length
+    def fill(chain):
+        @pl.loop(0, chain_waves // chunk)
+        def _(step):
+            first = pl.multiple_of(step * chunk, chunk)
+            turns = dot(waves[pl.ds(chain * chain_waves + first, chunk), :], pos_pieces)
+            for part, values in enumerate(turns_cos_sin(turns)):
+                where = pl.ds(chain * chain_rows + part * chain_waves + first, chunk)
+                rounded = values.astype(jnp.bfloat16)
+                phase[where, :] = rounded
+                sums[where, :] = dot(rounded, queries)
+
+    def cut(chain, stage):
+        device, _, _, length = plans[chain][stage]
+        place = chain * chain_rows + chain_rows - 2 * length
+        return pltpu.make_async_remote_copy(
+            src_ref=staged.at[pl.ds(place, length)],
+            dst_ref=landed.at[pl.ds(place, length)],
+            send_sem=cut_send.at[chain, stage],
+            recv_sem=cut_recv.at[chain, stage],
+            device_id=device,
+            device_id_type=MESH,
+        )
+
+    def start_cut(chain, stage):
+        _, _, send, length = plans[chain][stage]
+        place = chain * chain_rows + chain_rows - 2 * length
         staged[pl.ds(place, length), :] = sums[
             pl.ds(pl.multiple_of(send, piece_rows), length), :
         ].astype(jnp.bfloat16)
-        copy = pltpu.make_async_remote_copy(
-            src_ref=staged.at[pl.ds(place, length)],
-            dst_ref=landed.at[pl.ds(place, length)],
-            send_sem=cut_send.at[stage],
-            recv_sem=cut_recv.at[stage],
+        cut(chain, stage).start()
+
+    def end_cut(chain, stage):
+        cut(chain, stage).wait()
+        _, keep, _, length = plans[chain][stage]
+        place = chain * chain_rows + chain_rows - 2 * length
+        where = pl.ds(pl.multiple_of(keep, piece_rows), length)
+        sums[where, :] = sums[where, :] + landed[pl.ds(place, length), :].astype(jnp.float32)
+
+    def join(chain, stage):
+        device, keep, _, length = plans[chain][stage]
+        where = pl.ds(pl.multiple_of(keep, piece_rows), length)
+        return pltpu.make_async_remote_copy(
+            src_ref=filtered.at[where],
+            dst_ref=filtered.at[where],
+            send_sem=join_send.at[chain, stage],
+            recv_sem=join_recv.at[chain, stage],
             device_id=device,
             device_id_type=MESH,
         )
-        copy.start()
-        return copy
-
-    def add_cut(stage):
-        _, keep, _, length = plan[stage]
-        place = rows - 2 * length
-        where = pl.ds(pl.multiple_of(keep, piece_rows), length)
-        sums[where, :] = sums[where, :] + landed[pl.ds(place, length), :].astype(jnp.float32)
-
-    def join(stage):
-        device, keep, _, length = plan[stage]
-        where = pl.ds(pl.multiple_of(keep, piece_rows), length)
-        copy = pltpu.make_async_remote_copy(
-            src_ref=filtered.at[where],
-            dst_ref=filtered.at[where],
-            send_sem=join_send.at[stage],
-            recv_sem=join_recv.at[stage],
-            device_id=device,
-            device_id_type=MESH,
-        )
-        copy.start()
-        return copy
-
-    in_flight = cut(0)
+
+    def apply_gain(chain):
+        _, mine, _, mine_rows = plans[chain][-1]
+        scale = (atom_count * role_count * atoms_count) ** (-0.5) * ewald_scale
+        channel = kgain[...] * scale
+        where = pl.ds(pl.multiple_of(mine, piece_rows), mine_rows)
+        first_wave = chain * chain_waves + (mine - chain * chain_rows) % chain_waves
+        gain_rows = gain[pl.ds(pl.multiple_of(first_wave, piece_rows), mine_rows), :]
+        for part in range(width // 128):
+            lanes = pl.ds(part * 128, 128)
+            filtered[where, lanes] = (
+                sums[where, lanes] * gain_rows * channel[:, part * 128 : part * 128 + 128]
+            ).astype(jnp.bfloat16)
+
+    fill(0)
+    start_cut(0, 0)
     for copy in halo:
         copy.wait()
     halo = [send_brick(2 + number, *move) for number, move in enumerate(along)]
+    for chain in range(1, chains):
+        fill(chain)
+        start_cut(chain, 0)
 
     rbf_t[...] = flipped(w_rbf[...]).astype(jnp.bfloat16)
     filter_t[...] = flipped(w_filter[...]).astype(jnp.bfloat16)
@@ -243,9 +270,9 @@
     squares = dot(wave_part * wave_part, picks)
     gain[...] = jnp.exp(squares * (-1.0 / damping)) / squares
 
-    in_flight.wait()
-    add_cut(0)
-    in_flight = cut(1)
+    for chain in range(chains):
+        end_cut(chain, 0)
+        start_cut(chain, 1)
 
     @pl.loop(0, rows // chunk)
     def _(step):
@@ -293,52 +320,46 @@
         ).astype(jnp.bfloat16)
         messages[...] += dot(filter_t[...], inner) * source[0:width, :]
 
+    def cut_event(chain, stage):
+        end_cut(chain, stage)
+        if stage + 1 < stages:
+            start_cut(chain, stage + 1)
+        else:
+            apply_gain(chain)
+            join(chain, stage).start()
+
+    def join_event(chain, stage):
+        join(chain, stage).wait()
+        join(chain, stage - 1).start()
+
+    events = [
+        functools.partial(cut_event, chain, stage)
+        for stage in range(1, stages)
+        for chain in range(chains)
+    ] + [
+        functools.partial(join_event, chain, stage)
+        for stage in reversed(range(1, stages))
+        for chain in range(chains)
+    ]
+
+    for copy in halo:
+        copy.wait()
+    gather(0, wide_a)
     pairs = slot_count // 2
 
-    def short_range(first, last):
-        if last <= first:
-            return
-
-        @pl.loop(first, last)
-        def _(pair):
-            slot = pair * 2
-            gather(slot + 1, wide_b)
-            filter_slot(slot, wide_a)
-            gather(lax.rem(slot + 2, slot_count), wide_a)
-            filter_slot(slot + 1, wide_b)
-
-    stages = len(plan)
-    windows = 2 * stages - 2
-    share = [pairs * step // windows for step in range(windows + 1)]
-    for stage in range(1, stages):
-        if stage == 2:
-            for copy in halo:
-                copy.wait()
-            gather(0, wide_a)
-        if stage > 1:
-            short_range(share[stage - 2], share[stage - 1])
-        in_flight.wait()
-        add_cut(stage)
-        if stage + 1 < stages:
-            in_flight = cut(stage + 1)
-
-    _, mine, _, mine_rows = plan[-1]
-    scale = (atom_count * role_count * atoms_count) ** (-0.5) * ewald_scale
-    channel = kgain[...] * scale
-    where = pl.ds(pl.multiple_of(mine, piece_rows), mine_rows)
-    gain_rows = gain[pl.ds(pl.multiple_of(mine % wave_count, piece_rows), mine_rows), :]
-    for part in range(width // 128):
-        lanes = pl.ds(part * 128, 128)
-        filtered[where, lanes] = (
-            sums[where, lanes] * gain_rows * channel[:, part * 128 : part * 128 + 128]
-        ).astype(jnp.bfloat16)
-
-    for number, stage in enumerate(reversed(range(stages))):
-        in_flight = join(stage)
-        short_range(share[stages - 2 + number], share[stages - 1 + number])
-        if number == stages - 1:
-            short = jnp.transpose(messages[...]) * slot_count ** (-0.5)
-        in_flight.wait()
+    @pl.loop(0, pairs)
+    def _(pair):
+        slot = pair * 2
+        gather(slot + 1, wide_b)
+        filter_slot(slot, wide_a)
+        gather(lax.rem(slot + 2, slot_count), wide_a)
+        filter_slot(slot + 1, wide_b)
+        for number, event in enumerate(events):
+            pl.when(pair == number * pairs // len(events))(event)
+
+    short = jnp.transpose(messages[...]) * slot_count ** (-0.5)
+    for chain in range(chains):
+        join(chain, 0).wait()
 
     combined = (short + dot(phase_t[...], filtered[...])).astype(jnp.bfloat16)
     result[...] = (features[...].astype(jnp.float32) + dot(combined, w_out[...])).astype(
@@ -398,10 +419,10 @@
             pltpu.VMEM((width, atom_count), jnp.float32),
             pltpu.SemaphoreType.DMA((8,)),
             pltpu.SemaphoreType.DMA((8,)),
-            pltpu.SemaphoreType.DMA((stages,)),
-            pltpu.SemaphoreType.DMA((stages,)),
-            pltpu.SemaphoreType.DMA((stages,)),
-            pltpu.SemaphoreType.DMA((stages,)),
+            pltpu.SemaphoreType.DMA((2, stages)),
+            pltpu.SemaphoreType.DMA((2, stages)),
+            pltpu.SemaphoreType.DMA((2, stages)),
+            pltpu.SemaphoreType.DMA((2, stages)),
         ],
         compiler_params=pltpu.CompilerParams(
             collective_id=0, has_side_effects=True, vmem_limit_bytes=48 * 1024 * 1024

time: 69.9 us -> 62.2 us (0.89)
  Pallas kernels: 66.4 us -> 58.7 us
    pallas_call x1, Pallas kernels: 66.4 us -> 58.7 us  [local(): pl.pallas_call(functools.partial(block_kernel, role_count, atoms_count),...]
where the time goes in v3:
time: 62.2 us; the launch traced here: 61.9 us
  Pallas kernels  58.7 us (94%)
  local copies, waits for them, and re-layouts  2.31 us (4%)
  other arithmetic  0.8 us (1%)
    pallas_call x1, Pallas kernels, local(): pl.pallas_call(functools.partial(block_kernel, role_count, atoms_count),...  58.7 us
    unnamed x24, local copies, waits for them, and re-layouts  1.91 us

profile of v3, /device:TPU:0, one launch (start us, length us, event | category | flops | bytes accessed | tf_op | source)
XLA Modules:
  0.0 61.9 jit_solution(17618705907187655848)
XLA Ops:
  0.0 0.8 %convert.7 = bf16[3,2048]{1,0:T(4,128)(2,1)S(1)} convert(s32[3,2048]{1,0:T(4,128)} %param.16) | non-fusion elementwise | flops 6144 | bytes 36864 | tf_op jit(solution)/shard_map/convert.2
  0.8 0.3 copy.16
  1.1 0.0 copy-start.10
  1.1 0.0 copy-start
  1.1 0.0 copy-start.1
  1.1 0.0 copy-start.2
  1.2 0.0 copy-start.3
  1.2 0.0 copy-start.4
  1.2 0.0 copy-start.5
  1.2 0.0 copy-start.6
  1.2 0.0 copy-start.7
  1.2 0.0 copy-start.9
  1.2 0.1 pad_bitcast_fusion.waves
  1.3 0.5 copy-done.10
  1.8 0.0 copy-start.8
  1.8 0.2 copy-done
  2.0 0.1 copy-done.1
  2.1 0.1 copy-done.2
  2.2 0.1 copy-done.3
  2.2 0.1 copy-done.4
  2.3 0.0 copy-done.5
  2.3 0.0 copy-done.6
  2.3 0.0 copy-done.7
  2.3 0.0 copy-done.9
  2.3 0.2 copy-done.8
  2.6 58.7 %shard_map.118 = bf16[256,256]{1,0:T(8,128)(2,1)S(1)} custom-call(bf16[256,256]{1,0:T(8,128)(2,1)S(1)} %bitcast.12, f32[3,256]{1,0:T(4,128)S(1)} %bitcast.15, s32[32,256]{1,0:T(8,128)S(1)} %bitcast.13, s32[32,256]{1,0:T(8,128)S(1)} %bitcast.14, bf16[2048,16]{1,0:T(8,128)(2,1)S(1)} %pad_bitcast_fusion.waves, f32[1,256]{1,0:T(1,128)S(1)} %bitcast.16, ...), custom_call_target="tpu_custom_call" | custom-call | tf_op jit(solution)/shard_map/pallas_call | solution.py:397
  61.3 0.7 %copy.21 = bf16[1,1,256,256]{3,2,1,0:T(8,128)(2,1)} copy(bf16[1,1,256,256]{3,2,1,0:T(8,128)(2,1)S(1)} %bitcast.11) | data formatting | bytes 262144
  (2 shorter events, 0.0 us)
Async XLA Ops:
  1.1 0.7 %copy-start.10 = (f32[1,1,3,256]{3,1,2,0:T(1,128)S(1)}, f32[1,1,3,256]{3,1,2,0:T(1,128)}, u32[]{:S(2)}) copy-start(f32[1,1,3,256]{3,1,2,0:T(1,128)} %param.13) | copy-start | bytes 9220
  1.1 0.9 %copy-start = (bf16[1,1,256,256]{3,2,1,0:T(8,128)(2,1)S(1)}, bf16[1,1,256,256]{3,2,1,0:T(8,128)(2,1)}, u32[]{:S(2)}) copy-start(bf16[1,1,256,256]{3,2,1,0:T(8,128)(2,1)} %param.12) | copy-start | bytes 393220
  1.1 1.0 %copy-start.1 = (bf16[256,256]{1,0:T(8,128)(2,1)S(1)}, bf16[256,256]{1,0:T(8,128)(2,1)}, u32[]{:S(2)}) copy-start(bf16[256,256]{1,0:T(8,128)(2,1)} %w_in.1) | copy-start | bytes 393220
  1.1 1.0 %copy-start.2 = (bf16[256,256]{1,0:T(8,128)(2,1)S(1)}, bf16[256,256]{1,0:T(8,128)(2,1)}, u32[]{:S(2)}) copy-start(bf16[256,256]{1,0:T(8,128)(2,1)} %w_query.1) | copy-start | bytes 393220
  1.2 1.1 %copy-start.3 = (bf16[256,256]{1,0:T(8,128)(2,1)S(1)}, bf16[256,256]{1,0:T(8,128)(2,1)}, u32[]{:S(2)}) copy-start(bf16[256,256]{1,0:T(8,128)(2,1)} %w_filter.1) | copy-start | bytes 393220
  1.2 1.1 %copy-start.4 = (bf16[256,256]{1,0:T(8,128)(2,1)S(1)}, bf16[256,256]{1,0:T(8,128)(2,1)}, u32[]{:S(2)}) copy-start(bf16[256,256]{1,0:T(8,128)(2,1)} %w_out.1) | copy-start | bytes 393220
  1.2 1.1 %copy-start.5 = (s32[1,1,32,256]{3,2,1,0:T(8,128)S(1)}, s32[1,1,32,256]{3,2,1,0:T(8,128)}, u32[]{:S(2)}) copy-start(s32[1,1,32,256]{3,2,1,0:T(8,128)} %param.14) | copy-start | bytes 98308
  1.2 1.1 %copy-start.6 = (s32[1,1,32,256]{3,2,1,0:T(8,128)S(1)}, s32[1,1,32,256]{3,2,1,0:T(8,128)}, u32[]{:S(2)}) copy-start(s32[1,1,32,256]{3,2,1,0:T(8,128)} %param.15) | copy-start | bytes 98308
  1.2 1.1 %copy-start.7 = (bf16[64,256]{1,0:T(8,128)(2,1)S(1)}, bf16[64,256]{1,0:T(8,128)(2,1)}, u32[]{:S(2)}) copy-start(bf16[64,256]{1,0:T(8,128)(2,1)} %w_rbf.1) | copy-start | bytes 98308
  1.2 1.1 %copy-start.9 = (f32[256]{0:T(256)S(1)}, f32[256]{0:T(256)}, u32[]{:S(2)}) copy-start(f32[256]{0:T(256)} %param.21) | copy-start | bytes 3076
  1.8 0.8 %copy-start.8 = (f32[256]{0:T(256)S(1)}, f32[256]{0:T(256)}, u32[]{:S(2)}) copy-start(f32[256]{0:T(256)} %param.17) | copy-start | bytes 3076

commit v4 on v3

--- a/solution.py
+++ b/solution.py
@@ -81,7 +81,7 @@
     positions,
     neighbours,
     images,
-    waves,
+    wave,
     kgain,
     w_in,
     w_query,
@@ -90,6 +90,7 @@
     w_filter,
     w_out,
     result,
+    waves,
     table,
     pieces,
     phase,
@@ -117,7 +118,7 @@
     role, atoms = lax.axis_index("role"), lax.axis_index("atoms")
     atom_count, width = features.shape
     slot_count = neighbours.shape[0]
-    wave_count = waves.shape[0]
+    wave_count = wave.shape[1]
     basis_count = w_rbf.shape[0]
     rows = 2 * wave_count
     chains = 2 if rows // (role_count * atoms_count) >= 2 * piece_rows else 1
@@ -152,6 +153,9 @@
     pieces[3:6, :] = middle
     pieces[6:9, :] = rest - middle
     pos_pieces = pieces[...].astype(jnp.bfloat16)
+    waves[...] = jnp.zeros_like(waves)
+    for copy_number in range(3):
+        waves[copy_number * 3 : copy_number * 3 + 3, :] = wave[...].astype(jnp.float32)
     hidden = dot(features[...], w_in[...]).astype(jnp.bfloat16)
     table[4, 0:width, :] = flipped(hidden).astype(jnp.bfloat16)
     table[4, width : width + coord_rows, :] = pos_pieces
@@ -175,11 +179,14 @@
     queries = dot(features[...], w_query[...]).astype(jnp.bfloat16)
     chunk = 256
 
+    def wave_columns(first):
+        return flipped(waves[:, pl.ds(pl.multiple_of(first, chunk), chunk)]).astype(jnp.bfloat16)
+
     def fill(chain):
         @pl.loop(0, chain_waves // chunk)
         def _(step):
             first = pl.multiple_of(step * chunk, chunk)
-            turns = dot(waves[pl.ds(chain * chain_waves + first, chunk), :], pos_pieces)
+            turns = dot(wave_columns(chain * chain_waves + first), pos_pieces)
             for part, values in enumerate(turns_cos_sin(turns)):
                 where = pl.ds(chain * chain_rows + part * chain_waves + first, chunk)
                 rounded = values.astype(jnp.bfloat16)
@@ -263,19 +270,23 @@
         offsets[axis] = (part - 1).astype(jnp.float32) - own[axis : axis + 1, :]
     messages[...] = jnp.zeros_like(messages)
 
-    wave_part = waves[...]
     picks = jnp.where(
-        lax.broadcasted_iota(jnp.int32, (waves.shape[1], 128), 0) < 3, 1.0, 0.0
+        lax.broadcasted_iota(jnp.int32, (piece_rows, 128), 0) < 3, 1.0, 0.0
     ).astype(jnp.bfloat16)
-    squares = dot(wave_part * wave_part, picks)
-    gain[...] = jnp.exp(squares * (-1.0 / damping)) / squares
+
+    @pl.loop(0, wave_count // chunk)
+    def _(step):
+        first = pl.multiple_of(step * chunk, chunk)
+        columns = wave_columns(first)
+        squares = dot(columns * columns, picks)
+        gain[pl.ds(first, chunk), :] = jnp.exp(squares * (-1.0 / damping)) / squares
+
 
     for chain in range(chains):
         end_cut(chain, 0)
         start_cut(chain, 1)
 
-    @pl.loop(0, rows // chunk)
-    def _(step):
+    def turn_phase(step):
         first = pl.multiple_of(step * chunk, chunk)
         phase_t[:, pl.ds(first, chunk)] = flipped(phase[pl.ds(first, chunk), :]).astype(
             jnp.bfloat16
@@ -342,10 +353,17 @@
         for chain in range(chains)
     ]
 
+    early = chains
+    for event in events[:early]:
+        event()
     for copy in halo:
         copy.wait()
     gather(0, wide_a)
     pairs = slot_count // 2
+    late = events[early:]
+    turned = rows // chunk
+    for step in range(pairs, turned):
+        turn_phase(step)
 
     @pl.loop(0, pairs)
     def _(pair):
@@ -354,8 +372,12 @@
         filter_slot(slot, wide_a)
         gather(lax.rem(slot + 2, slot_count), wide_a)
         filter_slot(slot + 1, wide_b)
-        for number, event in enumerate(events):
-            pl.when(pair == number * pairs // len(events))(event)
+        if turned >= pairs:
+            turn_phase(pair)
+        else:
+            pl.when(pair < turned)(functools.partial(turn_phase, pair))
+        for number, event in enumerate(late):
+            pl.when(pair == number * (pairs - 1) // len(late))(event)
 
     short = jnp.transpose(messages[...]) * slot_count ** (-0.5)
     for chain in range(chains):
@@ -389,9 +411,6 @@
     slot_count = neighbours.shape[2]
     rows = 2 * wave_count
     stages = (role_count * atoms_count).bit_length() - 1
-    waves = jnp.transpose(
-        jnp.pad(jnp.concatenate([wave] * 3, axis=0), ((0, piece_rows - 9), (0, 0)))
-    ).astype(jnp.bfloat16)
     vmem = pl.BlockSpec(memory_space=pltpu.VMEM)
     full = width + coord_rows
     out = pl.pallas_call(
@@ -400,6 +419,7 @@
         in_specs=[vmem] * 12,
         out_specs=vmem,
         scratch_shapes=[
+            pltpu.VMEM((piece_rows, wave_count), jnp.float32),
             pltpu.VMEM((9, full, atom_count), jnp.bfloat16),
             pltpu.VMEM((piece_rows, atom_count), jnp.float32),
             pltpu.VMEM((rows, atom_count), jnp.bfloat16),
@@ -432,7 +452,7 @@
         positions[0, 0],
         neighbours[0, 0],
         images[0, 0],
-        waves,
+        wave,
         kgain[None, :],
         w_in,
         w_query,

time: 62.2 us -> 73.7 us (1.18)
  local copies, waits for them, and re-layouts: 2.31 us -> 9.58 us
  Pallas kernels: 58.7 us -> 63.6 us
  other arithmetic: 0.8 us -> 0 us
    unnamed x24 -> x26, local copies, waits for them, and re-layouts: 1.91 us -> 9.58 us
    pallas_call x1, Pallas kernels: 58.7 us -> 63.6 us  [local(): pl.pallas_call(functools.partial(block_kernel, role_count, atoms_count),...]
    another operation x1 -> x0, other arithmetic: 0.76 us -> none
where the time goes in v4:
time: 73.7 us; the launch traced here: 73.2 us
  Pallas kernels  63.6 us (86%)
  local copies, waits for them, and re-layouts  9.58 us (13%)
    pallas_call x1, Pallas kernels, local(): pl.pallas_call(functools.partial(block_kernel, role_count, atoms_count),...  63.6 us
    unnamed x26, local copies, waits for them, and re-layouts  9.58 us

profile of v4, /device:TPU:0, one launch (start us, length us, event | category | flops | bytes accessed | tf_op | source)
XLA Modules:
  0.0 73.2 jit_solution(14880489668076151137)
XLA Ops:
  0.0 0.0 copy-start.11
  0.0 0.7 copy-done.11
  0.7 0.0 copy-start.10
  0.7 0.0 copy-start.9
  0.7 0.7 copy-done.10
  1.4 0.0 copy-done.9
  1.4 0.0 copy-start
  1.4 0.9 %copy-done = bf16[1,1,256,256]{3,2,1,0:T(8,128)(2,1)S(1)} copy-done((bf16[1,1,256,256]{3,2,1,0:T(8,128)(2,1)S(1)}, bf16[1,1,256,256]{3,2,1,0:T(8,128)(2,1)}, u32[]{:S(2)}) %copy-start) | copy-done | bytes 131096
  2.3 0.0 copy-start.1
  2.3 0.9 %copy-done.1 = bf16[256,256]{1,0:T(8,128)(2,1)S(1)} copy-done((bf16[256,256]{1,0:T(8,128)(2,1)S(1)}, bf16[256,256]{1,0:T(8,128)(2,1)}, u32[]{:S(2)}) %copy-start.1) | copy-done | bytes 131096
  3.2 0.0 copy-start.2
  3.2 0.9 %copy-done.2 = bf16[256,256]{1,0:T(8,128)(2,1)S(1)} copy-done((bf16[256,256]{1,0:T(8,128)(2,1)S(1)}, bf16[256,256]{1,0:T(8,128)(2,1)}, u32[]{:S(2)}) %copy-start.2) | copy-done | bytes 131096
  4.1 0.0 copy-start.3
  4.1 0.9 %copy-done.3 = bf16[256,256]{1,0:T(8,128)(2,1)S(1)} copy-done((bf16[256,256]{1,0:T(8,128)(2,1)S(1)}, bf16[256,256]{1,0:T(8,128)(2,1)}, u32[]{:S(2)}) %copy-start.3) | copy-done | bytes 131096
  5.0 0.0 copy-start.4
  5.0 0.9 %copy-done.4 = bf16[256,256]{1,0:T(8,128)(2,1)S(1)} copy-done((bf16[256,256]{1,0:T(8,128)(2,1)S(1)}, bf16[256,256]{1,0:T(8,128)(2,1)}, u32[]{:S(2)}) %copy-start.4) | copy-done | bytes 131096
  5.9 0.0 copy-start.5
  5.9 0.8 %copy-done.5 = s32[1,1,32,256]{3,2,1,0:T(8,128)S(1)} copy-done((s32[1,1,32,256]{3,2,1,0:T(8,128)S(1)}, s32[1,1,32,256]{3,2,1,0:T(8,128)}, u32[]{:S(2)}) %copy-start.5) | copy-done | bytes 32792
  6.7 0.0 copy-start.6
  6.7 0.8 %copy-done.6 = s32[1,1,32,256]{3,2,1,0:T(8,128)S(1)} copy-done((s32[1,1,32,256]{3,2,1,0:T(8,128)S(1)}, s32[1,1,32,256]{3,2,1,0:T(8,128)}, u32[]{:S(2)}) %copy-start.6) | copy-done | bytes 32792
  7.4 0.0 copy-start.7
  7.4 0.8 %copy-done.7 = s32[3,2048]{1,0:T(4,128)S(1)} copy-done((s32[3,2048]{1,0:T(4,128)S(1)}, s32[3,2048]{1,0:T(4,128)}, u32[]{:S(2)}) %copy-start.7) | copy-done | bytes 24600
  8.2 0.0 copy-start.8
  8.2 0.8 %copy-done.8 = bf16[64,256]{1,0:T(8,128)(2,1)S(1)} copy-done((bf16[64,256]{1,0:T(8,128)(2,1)S(1)}, bf16[64,256]{1,0:T(8,128)(2,1)}, u32[]{:S(2)}) %copy-start.8) | copy-done | bytes 32792
  8.9 63.6 %shard_map.118 = bf16[256,256]{1,0:T(8,128)(2,1)S(1)} custom-call(bf16[256,256]{1,0:T(8,128)(2,1)S(1)} %bitcast.10, f32[3,256]{1,0:T(4,128)S(1)} %bitcast.13, s32[32,256]{1,0:T(8,128)S(1)} %bitcast.11, s32[32,256]{1,0:T(8,128)S(1)} %bitcast.12, s32[3,2048]{1,0:T(4,128)S(1)} %copy-done.7, f32[1,256]{1,0:T(1,128)S(1)} %bitcast.14, ...), custom_call_target="tpu_custom_call" | custom-call | tf_op jit(solution)/shard_map/pallas_call | solution.py:416
  72.5 0.7 copy.17
  (1 shorter events, 0.0 us)
Async XLA Ops:
  0.0 0.7 copy-start.11
  0.7 0.7 copy-start.10
  0.7 0.7 copy-start.9
  1.4 0.9 %copy-start = (bf16[1,1,256,256]{3,2,1,0:T(8,128)(2,1)S(1)}, bf16[1,1,256,256]{3,2,1,0:T(8,128)(2,1)}, u32[]{:S(2)}) copy-start(bf16[1,1,256,256]{3,2,1,0:T(8,128)(2,1)} %param.12) | copy-start | bytes 393220
  2.3 0.9 %copy-start.1 = (bf16[256,256]{1,0:T(8,128)(2,1)S(1)}, bf16[256,256]{1,0:T(8,128)(2,1)}, u32[]{:S(2)}) copy-start(bf16[256,256]{1,0:T(8,128)(2,1)} %w_in.1) | copy-start | bytes 393220
  3.2 0.9 %copy-start.2 = (bf16[256,256]{1,0:T(8,128)(2,1)S(1)}, bf16[256,256]{1,0:T(8,128)(2,1)}, u32[]{:S(2)}) copy-start(bf16[256,256]{1,0:T(8,128)(2,1)} %w_query.1) | copy-start | bytes 393220
  4.1 0.9 %copy-start.3 = (bf16[256,256]{1,0:T(8,128)(2,1)S(1)}, bf16[256,256]{1,0:T(8,128)(2,1)}, u32[]{:S(2)}) copy-start(bf16[256,256]{1,0:T(8,128)(2,1)} %w_filter.1) | copy-start | bytes 393220
  5.0 0.9 %copy-start.4 = (bf16[256,256]{1,0:T(8,128)(2,1)S(1)}, bf16[256,256]{1,0:T(8,128)(2,1)}, u32[]{:S(2)}) copy-start(bf16[256,256]{1,0:T(8,128)(2,1)} %w_out.1) | copy-start | bytes 393220
  5.9 0.8 %copy-start.5 = (s32[1,1,32,256]{3,2,1,0:T(8,128)S(1)}, s32[1,1,32,256]{3,2,1,0:T(8,128)}, u32[]{:S(2)}) copy-start(s32[1,1,32,256]{3,2,1,0:T(8,128)} %param.14) | copy-start | bytes 98308
  6.7 0.8 %copy-start.6 = (s32[1,1,32,256]{3,2,1,0:T(8,128)S(1)}, s32[1,1,32,256]{3,2,1,0:T(8,128)}, u32[]{:S(2)}) copy-start(s32[1,1,32,256]{3,2,1,0:T(8,128)} %param.15) | copy-start | bytes 98308
  7.4 0.8 %copy-start.7 = (s32[3,2048]{1,0:T(4,128)S(1)}, s32[3,2048]{1,0:T(4,128)}, u32[]{:S(2)}) copy-start(s32[3,2048]{1,0:T(4,128)} %wave.1) | copy-start | bytes 73732
  8.2 0.8 %copy-start.8 = (bf16[64,256]{1,0:T(8,128)(2,1)S(1)}, bf16[64,256]{1,0:T(8,128)(2,1)}, u32[]{:S(2)}) copy-start(bf16[64,256]{1,0:T(8,128)(2,1)} %w_rbf.1) | copy-start | bytes 98308

commit v5 on v3

--- a/solution.py
+++ b/solution.py
@@ -274,12 +274,21 @@
         end_cut(chain, 0)
         start_cut(chain, 1)
 
+    square_shape = (atom_count, atom_count)
+    on_diagonal = lax.broadcasted_iota(jnp.int32, square_shape, 0) == lax.broadcasted_iota(
+        jnp.int32, square_shape, 1
+    )
+    identity = jnp.where(on_diagonal, 1.0, 0.0).astype(jnp.bfloat16)
+
     @pl.loop(0, rows // chunk)
     def _(step):
         first = pl.multiple_of(step * chunk, chunk)
-        phase_t[:, pl.ds(first, chunk)] = flipped(phase[pl.ds(first, chunk), :]).astype(
-            jnp.bfloat16
-        )
+        phase_t[:, pl.ds(first, chunk)] = lax.dot_general(
+            identity,
+            phase[pl.ds(first, chunk), :],
+            (((1,), (1,)), ((), ())),
+            preferred_element_type=jnp.float32,
+        ).astype(jnp.bfloat16)
 
     lane_atoms = lax.broadcasted_iota(jnp.int32, (atom_count, atom_count), 0).astype(
         jnp.float32
@@ -342,10 +351,14 @@
         for chain in range(chains)
     ]
 
+    early = chains
+    for event in events[:early]:
+        event()
     for copy in halo:
         copy.wait()
     gather(0, wide_a)
     pairs = slot_count // 2
+    late = events[early:]
 
     @pl.loop(0, pairs)
     def _(pair):
@@ -354,8 +367,8 @@
         filter_slot(slot, wide_a)
         gather(lax.rem(slot + 2, slot_count), wide_a)
         filter_slot(slot + 1, wide_b)
-        for number, event in enumerate(events):
-            pl.when(pair == number * pairs // len(events))(event)
+        for number, event in enumerate(late):
+            pl.when(pair == number * (pairs - 1) // len(late))(event)
 
     short = jnp.transpose(messages[...]) * slot_count ** (-0.5)
     for chain in range(chains):

time: 62.2 us -> 63.3 us (1.018)
  Pallas kernels: 58.7 us -> 59.9 us
    pallas_call x1, Pallas kernels: 58.7 us -> 59.9 us  [local(): pl.pallas_call(functools.partial(block_kernel, role_count, atoms_count),...]
where the time goes in v5:
time: 63.3 us; the launch traced here: 63.1 us
  Pallas kernels  59.9 us (95%)
  local copies, waits for them, and re-layouts  2.31 us (4%)
  other arithmetic  0.8 us (1%)
    pallas_call x1, Pallas kernels, local(): pl.pallas_call(functools.partial(block_kernel, role_count, atoms_count),...  59.9 us
    unnamed x24, local copies, waits for them, and re-layouts  1.91 us

profile of v5, /device:TPU:0, one launch (start us, length us, event | category | flops | bytes accessed | tf_op | source)
XLA Modules:
  0.0 63.1 jit_solution(3421337282921252389)
XLA Ops:
  0.0 0.8 %convert.7 = bf16[3,2048]{1,0:T(4,128)(2,1)S(1)} convert(s32[3,2048]{1,0:T(4,128)} %param.16) | non-fusion elementwise | flops 6144 | bytes 36864 | tf_op jit(solution)/shard_map/convert.2
  0.8 0.3 copy.16
  1.1 0.0 copy-start.10
  1.1 0.0 copy-start
  1.1 0.0 copy-start.1
  1.1 0.0 copy-start.2
  1.2 0.0 copy-start.3
  1.2 0.0 copy-start.4
  1.2 0.0 copy-start.5
  1.2 0.0 copy-start.6
  1.2 0.0 copy-start.7
  1.2 0.0 copy-start.9
  1.2 0.1 pad_bitcast_fusion.waves
  1.3 0.5 copy-done.10
  1.8 0.0 copy-start.8
  1.8 0.2 copy-done
  2.0 0.1 copy-done.1
  2.1 0.1 copy-done.2
  2.2 0.1 copy-done.3
  2.2 0.1 copy-done.4
  2.3 0.0 copy-done.5
  2.3 0.0 copy-done.6
  2.3 0.0 copy-done.7
  2.3 0.0 copy-done.9
  2.3 0.2 copy-done.8
  2.6 59.9 %shard_map.118 = bf16[256,256]{1,0:T(8,128)(2,1)S(1)} custom-call(bf16[256,256]{1,0:T(8,128)(2,1)S(1)} %bitcast.12, f32[3,256]{1,0:T(4,128)S(1)} %bitcast.15, s32[32,256]{1,0:T(8,128)S(1)} %bitcast.13, s32[32,256]{1,0:T(8,128)S(1)} %bitcast.14, bf16[2048,16]{1,0:T(8,128)(2,1)S(1)} %pad_bitcast_fusion.waves, f32[1,256]{1,0:T(1,128)S(1)} %bitcast.16, ...), custom_call_target="tpu_custom_call" | custom-call | tf_op jit(solution)/shard_map/pallas_call | solution.py:410
  62.5 0.7 %copy.21 = bf16[1,1,256,256]{3,2,1,0:T(8,128)(2,1)} copy(bf16[1,1,256,256]{3,2,1,0:T(8,128)(2,1)S(1)} %bitcast.11) | data formatting | bytes 262144
  (2 shorter events, 0.0 us)
Async XLA Ops:
  1.1 0.7 %copy-start.10 = (f32[1,1,3,256]{3,1,2,0:T(1,128)S(1)}, f32[1,1,3,256]{3,1,2,0:T(1,128)}, u32[]{:S(2)}) copy-start(f32[1,1,3,256]{3,1,2,0:T(1,128)} %param.13) | copy-start | bytes 9220
  1.1 0.9 %copy-start = (bf16[1,1,256,256]{3,2,1,0:T(8,128)(2,1)S(1)}, bf16[1,1,256,256]{3,2,1,0:T(8,128)(2,1)}, u32[]{:S(2)}) copy-start(bf16[1,1,256,256]{3,2,1,0:T(8,128)(2,1)} %param.12) | copy-start | bytes 393220
  1.1 1.0 %copy-start.1 = (bf16[256,256]{1,0:T(8,128)(2,1)S(1)}, bf16[256,256]{1,0:T(8,128)(2,1)}, u32[]{:S(2)}) copy-start(bf16[256,256]{1,0:T(8,128)(2,1)} %w_in.1) | copy-start | bytes 393220
  1.1 1.0 %copy-start.2 = (bf16[256,256]{1,0:T(8,128)(2,1)S(1)}, bf16[256,256]{1,0:T(8,128)(2,1)}, u32[]{:S(2)}) copy-start(bf16[256,256]{1,0:T(8,128)(2,1)} %w_query.1) | copy-start | bytes 393220
  1.2 1.1 %copy-start.3 = (bf16[256,256]{1,0:T(8,128)(2,1)S(1)}, bf16[256,256]{1,0:T(8,128)(2,1)}, u32[]{:S(2)}) copy-start(bf16[256,256]{1,0:T(8,128)(2,1)} %w_filter.1) | copy-start | bytes 393220
  1.2 1.1 %copy-start.4 = (bf16[256,256]{1,0:T(8,128)(2,1)S(1)}, bf16[256,256]{1,0:T(8,128)(2,1)}, u32[]{:S(2)}) copy-start(bf16[256,256]{1,0:T(8,128)(2,1)} %w_out.1) | copy-start | bytes 393220
  1.2 1.1 %copy-start.5 = (s32[1,1,32,256]{3,2,1,0:T(8,128)S(1)}, s32[1,1,32,256]{3,2,1,0:T(8,128)}, u32[]{:S(2)}) copy-start(s32[1,1,32,256]{3,2,1,0:T(8,128)} %param.14) | copy-start | bytes 98308
  1.2 1.1 %copy-start.6 = (s32[1,1,32,256]{3,2,1,0:T(8,128)S(1)}, s32[1,1,32,256]{3,2,1,0:T(8,128)}, u32[]{:S(2)}) copy-start(s32[1,1,32,256]{3,2,1,0:T(8,128)} %param.15) | copy-start | bytes 98308
  1.2 1.1 %copy-start.7 = (bf16[64,256]{1,0:T(8,128)(2,1)S(1)}, bf16[64,256]{1,0:T(8,128)(2,1)}, u32[]{:S(2)}) copy-start(bf16[64,256]{1,0:T(8,128)(2,1)} %w_rbf.1) | copy-start | bytes 98308
  1.2 1.1 %copy-start.9 = (f32[256]{0:T(256)S(1)}, f32[256]{0:T(256)}, u32[]{:S(2)}) copy-start(f32[256]{0:T(256)} %param.21) | copy-start | bytes 3076
  1.8 0.8 %copy-start.8 = (f32[256]{0:T(256)S(1)}, f32[256]{0:T(256)}, u32[]{:S(2)}) copy-start(f32[256]{0:T(256)} %param.17) | copy-start | bytes 3076

commit v6 on v5

--- a/solution.py
+++ b/solution.py
@@ -351,7 +351,7 @@
         for chain in range(chains)
     ]
 
-    early = chains
+    early = 0
     for event in events[:early]:
         event()
     for copy in halo:
@@ -368,7 +368,7 @@
         gather(lax.rem(slot + 2, slot_count), wide_a)
         filter_slot(slot + 1, wide_b)
         for number, event in enumerate(late):
-            pl.when(pair == number * (pairs - 1) // len(late))(event)
+            pl.when(pair == number * pairs // len(late))(event)
 
     short = jnp.transpose(messages[...]) * slot_count ** (-0.5)
     for chain in range(chains):

time: 63.3 us -> 62.1 us (0.981)
  Pallas kernels: 59.9 us -> 58.6 us
    pallas_call x1, Pallas kernels: 59.9 us -> 58.6 us  [local(): pl.pallas_call(functools.partial(block_kernel, role_count, atoms_count),...]
where the time goes in v6:
time: 62.1 us; the launch traced here: 61.8 us
  Pallas kernels  58.6 us (94%)
  local copies, waits for them, and re-layouts  2.31 us (4%)
  other arithmetic  0.8 us (1%)
    pallas_call x1, Pallas kernels, local(): pl.pallas_call(functools.partial(block_kernel, role_count, atoms_count),...  58.6 us
    unnamed x24, local copies, waits for them, and re-layouts  1.91 us

profile of v6, /device:TPU:0, one launch (start us, length us, event | category | flops | bytes accessed | tf_op | source)
XLA Modules:
  0.0 61.8 jit_solution(4591418723061161880)
XLA Ops:
  0.0 0.8 %convert.7 = bf16[3,2048]{1,0:T(4,128)(2,1)S(1)} convert(s32[3,2048]{1,0:T(4,128)} %param.16) | non-fusion elementwise | flops 6144 | bytes 36864 | tf_op jit(solution)/shard_map/convert.2
  0.8 0.3 copy.16
  1.1 0.0 copy-start.10
  1.1 0.0 copy-start
  1.1 0.0 copy-start.1
  1.1 0.0 copy-start.2
  1.2 0.0 copy-start.3
  1.2 0.0 copy-start.4
  1.2 0.0 copy-start.5
  1.2 0.0 copy-start.6
  1.2 0.0 copy-start.7
  1.2 0.0 copy-start.9
  1.2 0.1 pad_bitcast_fusion.waves
  1.3 0.5 copy-done.10
  1.8 0.0 copy-start.8
  1.8 0.2 copy-done
  2.0 0.1 copy-done.1
  2.1 0.1 copy-done.2
  2.2 0.1 copy-done.3
  2.2 0.1 copy-done.4
  2.3 0.0 copy-done.5
  2.3 0.0 copy-done.6
  2.3 0.0 copy-done.7
  2.3 0.0 copy-done.9
  2.3 0.2 copy-done.8
  2.6 58.6 %shard_map.118 = bf16[256,256]{1,0:T(8,128)(2,1)S(1)} custom-call(bf16[256,256]{1,0:T(8,128)(2,1)S(1)} %bitcast.12, f32[3,256]{1,0:T(4,128)S(1)} %bitcast.15, s32[32,256]{1,0:T(8,128)S(1)} %bitcast.13, s32[32,256]{1,0:T(8,128)S(1)} %bitcast.14, bf16[2048,16]{1,0:T(8,128)(2,1)S(1)} %pad_bitcast_fusion.waves, f32[1,256]{1,0:T(1,128)S(1)} %bitcast.16, ...), custom_call_target="tpu_custom_call" | custom-call | tf_op jit(solution)/shard_map/pallas_call | solution.py:410
  61.2 0.7 %copy.21 = bf16[1,1,256,256]{3,2,1,0:T(8,128)(2,1)} copy(bf16[1,1,256,256]{3,2,1,0:T(8,128)(2,1)S(1)} %bitcast.11) | data formatting | bytes 262144
  (2 shorter events, 0.0 us)
Async XLA Ops:
  1.1 0.7 %copy-start.10 = (f32[1,1,3,256]{3,1,2,0:T(1,128)S(1)}, f32[1,1,3,256]{3,1,2,0:T(1,128)}, u32[]{:S(2)}) copy-start(f32[1,1,3,256]{3,1,2,0:T(1,128)} %param.13) | copy-start | bytes 9220
  1.1 0.9 %copy-start = (bf16[1,1,256,256]{3,2,1,0:T(8,128)(2,1)S(1)}, bf16[1,1,256,256]{3,2,1,0:T(8,128)(2,1)}, u32[]{:S(2)}) copy-start(bf16[1,1,256,256]{3,2,1,0:T(8,128)(2,1)} %param.12) | copy-start | bytes 393220
  1.1 1.0 %copy-start.1 = (bf16[256,256]{1,0:T(8,128)(2,1)S(1)}, bf16[256,256]{1,0:T(8,128)(2,1)}, u32[]{:S(2)}) copy-start(bf16[256,256]{1,0:T(8,128)(2,1)} %w_in.1) | copy-start | bytes 393220
  1.1 1.0 %copy-start.2 = (bf16[256,256]{1,0:T(8,128)(2,1)S(1)}, bf16[256,256]{1,0:T(8,128)(2,1)}, u32[]{:S(2)}) copy-start(bf16[256,256]{1,0:T(8,128)(2,1)} %w_query.1) | copy-start | bytes 393220
  1.2 1.1 %copy-start.3 = (bf16[256,256]{1,0:T(8,128)(2,1)S(1)}, bf16[256,256]{1,0:T(8,128)(2,1)}, u32[]{:S(2)}) copy-start(bf16[256,256]{1,0:T(8,128)(2,1)} %w_filter.1) | copy-start | bytes 393220
  1.2 1.1 %copy-start.4 = (bf16[256,256]{1,0:T(8,128)(2,1)S(1)}, bf16[256,256]{1,0:T(8,128)(2,1)}, u32[]{:S(2)}) copy-start(bf16[256,256]{1,0:T(8,128)(2,1)} %w_out.1) | copy-start | bytes 393220
  1.2 1.1 %copy-start.5 = (s32[1,1,32,256]{3,2,1,0:T(8,128)S(1)}, s32[1,1,32,256]{3,2,1,0:T(8,128)}, u32[]{:S(2)}) copy-start(s32[1,1,32,256]{3,2,1,0:T(8,128)} %param.14) | copy-start | bytes 98308
  1.2 1.1 %copy-start.6 = (s32[1,1,32,256]{3,2,1,0:T(8,128)S(1)}, s32[1,1,32,256]{3,2,1,0:T(8,128)}, u32[]{:S(2)}) copy-start(s32[1,1,32,256]{3,2,1,0:T(8,128)} %param.15) | copy-start | bytes 98308
  1.2 1.1 %copy-start.7 = (bf16[64,256]{1,0:T(8,128)(2,1)S(1)}, bf16[64,256]{1,0:T(8,128)(2,1)}, u32[]{:S(2)}) copy-start(bf16[64,256]{1,0:T(8,128)(2,1)} %w_rbf.1) | copy-start | bytes 98308
  1.2 1.1 %copy-start.9 = (f32[256]{0:T(256)S(1)}, f32[256]{0:T(256)}, u32[]{:S(2)}) copy-start(f32[256]{0:T(256)} %param.21) | copy-start | bytes 3076
  1.8 0.8 %copy-start.8 = (f32[256]{0:T(256)S(1)}, f32[256]{0:T(256)}, u32[]{:S(2)}) copy-start(f32[256]{0:T(256)} %param.17) | copy-start | bytes 3076
